TPU v7x, 128 devices: a whole 4x4x4 slice. The times are simulated.
128 devices in a mesh: ctx: 16 (over z, x), enc: 8 (over y, core).
Axes of the slice: x: 4, y: 4, z: 4, core: 2. Of those that a mesh axis runs over, the one named last changes fastest.
Arguments:
- queries: bfloat16 [4096, 8192], P('ctx', 'enc'), may hold values from -6 to 6
- out_grad: bfloat16 [4096, 8192], P('ctx', 'enc'), may hold values from -6 to 6
- nbr_states: bfloat16 [64, 128, 2048], P('ctx', None, 'enc'), may hold values from -6 to 6
- key_weight: bfloat16 [2048, 8192], P('ctx', 'enc'), may hold values from -0.125 to 0.125
- value_weight: bfloat16 [2048, 8192], P('ctx', 'enc'), may hold values from -0.125 to 0.125
- q_gain: float32 [8192], P('enc'), may hold values from 0.25 to 1.75
- k_gain: float32 [8192], P('enc'), may hold values from 0.25 to 1.75
- nbr_owner: int32 [64, 2], replicated, may hold values from 0 to 15, all different within a row; in each aligned block of 4 rows (0 to 3, 4 to 7, ...) at most 2 rows name the same one
- nbr_slot: int32 [64, 2], replicated, may hold values from 0 to 3
Outputs:
- query_grad: bfloat16 [4096, 8192], P('ctx', 'enc')
- state_grad: float32 [64, 128, 2048], P('ctx', None, 'enc')
Inputs may be any that keep to these rules, and one draw needn't show every extreme that they name: `nbr_owner`: within the 4 spans of one ctx index (aligned blocks of spans), no owner is named more than 2 times, a bound that some block reaches; a span's two neighbours have different owners.
All inputs are finite; a program needn't handle non-finite values.
Results may differ from a plain program's by a relative error of at most 0.018.
Values may be sent and summed in bfloat16 or wider, within the bound.
A program may use at most 192 MiB of HBM per device.

v0:
```python
import jax
import jax.numpy as jnp
from jax import lax
from jax.sharding import PartitionSpec as P

DH = 128
SPAN = 64
NT = 128
CAP = 2


PRECISE = lax.Precision.HIGHEST
EPSILON = 1e-06
LOG_BASE = 9.210340371976184


def from_behind(value, axis, steps):
    count = lax.axis_size(axis)
    leading, last = (max(0, -steps), min(count, count - steps))
    return lax.ppermute(value, axis, [(source, source + steps) for source in range(leading, last)])


def normalize(tensor):
    return tensor * lax.rsqrt(jnp.mean(tensor * tensor, axis=-1, keepdims=True) + EPSILON)


def rotate(tensor, positions):
    halved = tensor.shape[-1] // 2
    exponents = jnp.arange(halved).astype(jnp.float32)
    frequency = jnp.exp(exponents * (-2.0 * LOG_BASE / tensor.shape[-1]))
    angles = positions.astype(jnp.float32)[:, None] * frequency[None, :]
    cosine = jnp.cos(angles)[:, None, :]
    sine_part = jnp.sin(angles)[:, None, :]
    first_half = tensor[..., :halved]
    second_half = tensor[..., halved:]
    return jnp.concatenate(
        [
            first_half * cosine - second_half * sine_part,
            first_half * sine_part + second_half * cosine,
        ],
        axis=-1,
    )


def attend(query_win, key_win, value_win, query_scale, key_scale):
    query_rot = rotate(normalize(query_win) * query_scale, jnp.arange(query_win.shape[1]))
    key_rot = rotate(normalize(key_win) * key_scale, jnp.arange(key_win.shape[1]) % NT)
    scores = jnp.einsum("wqhd,wkhd->whqk", query_rot, key_rot, precision=PRECISE) * query_win.shape[
        -1
    ] ** (-0.5)
    weights = jax.nn.softmax(scores, axis=-1)
    return jnp.einsum("whqk,wkhd->wqhd", weights, value_win, precision=PRECISE)


def shards(
    queries, out_grad, nbr_states, key_weight, value_weight, q_gain, k_gain, nbr_owner, nbr_slot
):
    members = lax.axis_size("ctx")
    place = lax.axis_index("ctx")
    length = queries.shape[0]
    span_count = length // SPAN
    references = 2 * span_count
    stored = nbr_states.shape[0]
    feature_width = nbr_states.shape[2]
    heads_width = queries.shape[1]
    head_count = heads_width // DH
    key_full, value_full = (
        lax.all_gather(key_weight, "ctx", axis=0, tiled=True),
        lax.all_gather(value_weight, "ctx", axis=0, tiled=True),
    )
    owner_table = nbr_owner.reshape(members, references)
    slot_table = nbr_slot.reshape(members, references)
    indices = jnp.arange(references)
    earlier = indices[None, :] < indices[:, None]
    matched = owner_table[:, :, None] == owner_table[:, None, :]
    ranking = jnp.sum(matched & earlier[None], axis=2)
    slot_numbers = jnp.arange(CAP)
    picked = (owner_table[:, None, :] == place) & (
        ranking[:, None, :] == slot_numbers[None, :, None]
    )
    filled = jnp.any(picked, axis=2).reshape(-1)
    local_index = jnp.sum(jnp.where(picked, slot_table[:, None, :], 0), axis=2).reshape(-1)
    outgoing = jnp.take(nbr_states, local_index, axis=0)
    outgoing = jnp.where(filled[:, None, None], outgoing, jnp.zeros_like(outgoing))
    outgoing = outgoing.reshape(members, CAP, NT, feature_width)
    incoming = lax.all_to_all(outgoing, "ctx", split_axis=0, concat_axis=0, tiled=True)
    my_owners = lax.dynamic_index_in_dim(owner_table, place, 0, keepdims=False)
    my_ranking = lax.dynamic_index_in_dim(ranking, place, 0, keepdims=False)
    flat_position = my_owners * CAP + my_ranking
    received = jnp.take(incoming.reshape(members * CAP, NT, feature_width), flat_position, axis=0)
    block_rows = lax.all_gather(received, "enc", axis=2, tiled=True)
    row_total = block_rows.shape[2]
    flattened = block_rows.reshape(-1, row_total)
    key_rows = key_full
    value_rows = value_full
    key_total = jnp.dot(flattened, key_rows, preferred_element_type=jnp.float32)
    value_total = jnp.dot(flattened, value_rows, preferred_element_type=jnp.float32)
    key_pre = key_total.astype(jnp.bfloat16).reshape(span_count, 2 * NT, heads_width)
    value_pre = value_total.astype(jnp.bfloat16).reshape(span_count, 2 * NT, heads_width)
    query_scale = q_gain.reshape(head_count, DH)
    key_scale = k_gain.reshape(head_count, DH)

    def attend_here(query_arg, key_arg, value_arg):
        return attend(query_arg, key_arg, value_arg, query_scale, key_scale)

    prev_key, prev_value = from_behind((key_pre[-1], value_pre[-1]), "ctx", 1)
    key_win = (
        jnp.concatenate([prev_key[None], key_pre])
        .astype(jnp.float32)
        .reshape(span_count + 1, 2 * NT, head_count, DH)
    )
    value_win = (
        jnp.concatenate([prev_value[None], value_pre])
        .astype(jnp.float32)
        .reshape(span_count + 1, 2 * NT, head_count, DH)
    )
    leading = jnp.zeros((1, heads_width), jnp.bfloat16)
    trailing = jnp.zeros((SPAN - 1, heads_width), jnp.bfloat16)
    query_win = (
        jnp.concatenate([leading, queries, trailing])
        .astype(jnp.float32)
        .reshape(span_count + 1, SPAN, head_count, DH)
    )
    grad_win = (
        jnp.concatenate([leading, out_grad, trailing])
        .astype(jnp.float32)
        .reshape(span_count + 1, SPAN, head_count, DH)
    )
    attended, pullback = jax.vjp(attend_here, query_win, key_win, value_win)
    grad_query, grad_key, grad_value = pullback(grad_win)
    query_grad = grad_query.reshape(-1, heads_width)[1 : 1 + length].astype(jnp.bfloat16)
    late_key, late_value = (
        from_behind(grad_key[0].astype(jnp.bfloat16), "ctx", -1).astype(jnp.float32),
        from_behind(grad_value[0].astype(jnp.bfloat16), "ctx", -1).astype(jnp.float32),
    )
    span_key_grad = grad_key[1:].at[-1].add(late_key)
    span_value_grad = grad_value[1:].at[-1].add(late_value)
    key_grad = span_key_grad.reshape(references * NT, heads_width).astype(jnp.bfloat16)
    value_grad = span_value_grad.reshape(references * NT, heads_width).astype(jnp.bfloat16)
    contract = (((1,), (1,)), ((), ()))
    placing_mask = flat_position[None, :] == jnp.arange(members * CAP)[:, None]
    collect_mask = (local_index[None, :] == jnp.arange(stored)[:, None]) & filled[None, :]
    key_rows = key_full
    value_rows = value_full
    shares = lax.psum_scatter(
        (
            lax.dot_general(key_rows, key_grad, contract, preferred_element_type=jnp.float32)
            + lax.dot_general(value_rows, value_grad, contract, preferred_element_type=jnp.float32)
        ).astype(jnp.bfloat16),
        "enc",
        scatter_dimension=0,
        tiled=True,
    ).astype(jnp.float32)
    ref_grads = jnp.transpose(shares.reshape(feature_width, references, NT), (1, 2, 0))
    placing = placing_mask.astype(jnp.float32)
    returning = jnp.dot(
        placing, ref_grads.reshape(references, NT * feature_width), precision=PRECISE
    )
    arrived = lax.all_to_all(
        returning.reshape(members, CAP, NT, feature_width).astype(jnp.bfloat16),
        "ctx",
        split_axis=0,
        concat_axis=0,
        tiled=True,
    ).astype(jnp.float32)
    collect = collect_mask.astype(jnp.float32)
    state_grad = jnp.dot(
        collect, arrived.reshape(members * CAP, NT * feature_width), precision=PRECISE
    )
    state_grad = state_grad.reshape(stored, NT, feature_width)
    return (query_grad, state_grad)


def solution(mesh):
    in_specs = (
        P("ctx", "enc"),
        P("ctx", "enc"),
        P("ctx", None, "enc"),
        P("ctx", "enc"),
        P("ctx", "enc"),
        P("enc"),
        P("enc"),
        P(),
        P(),
    )
    out_specs = (P("ctx", "enc"), P("ctx", None, "enc"))
    return jax.shard_map(shards, mesh=mesh, in_specs=in_specs, out_specs=out_specs, check_vma=False)
```

profile of v0, /device:TPU:25, one launch (start us, length us, event | category | flops | bytes accessed | tf_op | source)
XLA Modules:
  0.0 393.9 jit_solution(13062372083840744862)
XLA Ops:
  11.1 1.7 select_select_fusion
  12.8 7.7 %all-to-all-start = ((bf16[16,2,128,256]{3,2,1,0:T(8,128)(2,1)}), bf16[16,2,128,256]{3,2,1,0:T(8,128)(2,1)S(1)}, u32[]{:S(2)}, u32[]{:S(2)}) async-start(bf16[16,2,128,256]{3,2,1,0:T(8,128)(2,1)} %select_select_fusion), calls=%async_computation | async-start | bytes 4194304 | tf_op jit(solution)/shard_map/all_to_all | solution.py:86
  20.9 34.4 %all-to-all-done = bf16[16,2,128,256]{3,2,1,0:T(8,128)(2,1)S(1)} async-done(((bf16[16,2,128,256]{3,2,1,0:T(8,128)(2,1)}), bf16[16,2,128,256]{3,2,1,0:T(8,128)(2,1)S(1)}, u32[]{:S(2)}, u32[]{:S(2)}) %all-to-all-start) | async-done | bytes 2097184 | tf_op jit(solution)/shard_map/all_to_all | solution.py:86
  62.7 18.7 %all-gather.6.cloned.1.call-done = bf16[2048,1024]{1,0:T(8,128)(2,1)} async-done(((bf16[128,1024]{1,0:T(8,128)(2,1)}), bf16[2048,1024]{1,0:T(8,128)(2,1)}) %all-gather.6.cloned.1.call-update) | async-done | bytes 4194320 | tf_op jit(solution)/shard_map/all_gather | solution.py:69
  81.4 37.7 %all-gather.4.cloned.1.call-done = bf16[8,128,2048]{2,1,0:T(8,128)(2,1)} async-done(((bf16[8,128,256]{2,1,0:T(8,128)(2,1)}), bf16[8,128,2048]{2,1,0:T(8,128)(2,1)}) %all-gather.4.cloned.1.call-update) | async-done | bytes 4194320 | tf_op jit(solution)/shard_map/all_gather | solution.py:91
  119.0 7.9 %convolution_convert_fusion.2 = bf16[1024,1024]{1,0:T(8,128)(2,1)S(1)} fusion(bf16[1024,2048]{1,0:T(8,128)(2,1)} %bitcast.143, bf16[2048,1024]{1,0:T(8,128)(2,1)} %all-gather.6.cloned.1.call-done), kind=kOutput, calls=%fused_computation.43 | convolution fusion | flops 4296015872 | bytes 10485760 | tf_op jit(solution)/shard_map/dot_general | solution.py:97
  129.2 45.0 %all-gather.8.cloned.1.call-done = bf16[2048,1024]{1,0:T(8,128)(2,1)} async-done(((bf16[128,1024]{1,0:T(8,128)(2,1)}), bf16[2048,1024]{1,0:T(8,128)(2,1)}) %all-gather.8.cloned.1.call-update) | async-done | bytes 4194320 | tf_op jit(solution)/shard_map/all_gather | solution.py:68
  174.1 7.9 %convolution_convert_fusion.1 = bf16[1024,1024]{1,0:T(8,128)(2,1)S(1)} fusion(bf16[1024,2048]{1,0:T(8,128)(2,1)} %bitcast.144, bf16[2048,1024]{1,0:T(8,128)(2,1)} %all-gather.8.cloned.1.call-done), kind=kOutput, calls=%fused_computation.42 | convolution fusion | flops 4296015872 | bytes 10485760 | tf_op jit(solution)/shard_map/dot_general | solution.py:96
  182.1 3.1 collective-permute-start.1
  185.3 3.6 collective-permute-start
  189.0 2.0 multiply_subtract_fusion.1
  193.9 1.8 copy.147
  196.0 11.1 %collective-permute-done = bf16[256,1024]{1,0:T(8,128)(2,1)S(1)} collective-permute-done((bf16[256,1024]{1,0:T(8,128)(2,1)}, bf16[256,1024]{1,0:T(8,128)(2,1)S(1)}, u32[]{:S(2)}, u32[]{:S(2)}) %collective-permute-start) | collective-permute-done | bytes 524320 | tf_op jit(solution)/shard_map/ppermute | solution.py:20
  211.3 4.9 %multiply_subtract_fusion = (f32[5,256,8,64]{3,1,2,0:T(8,128)S(1)}, f32[5,256,8,64]{3,1,2,0:T(8,128)}) fusion(f32[5,256,8,128]{3,1,2,0:T(8,128)S(1)} %fusion.1, f32[256,64]{1,0:T(8,128)} %get-tuple-element.51, f32[256,64]{1,0:T(8,128)S(1)} %get-tuple-element.50), kind=kLoop, calls=%fused_computation.16 | loop fusion | flops 3932160 | bytes 10616832 | tf_op jit(solution)/shard_map/jvp()/sub | solution.py:38
  216.2 11.7 %multiply_reduce_fusion.1 = (f32[5,8,64]{2,1,0:T(8,128)S(1)}, f32[5,8,64,256]{3,2,1,0:T(8,128)S(1)}) fusion(f32[5,256,8,64]{3,1,2,0:T(8,128)} %get-tuple-element.43, f32[5,256,8,64]{3,1,2,0:T(8,128)S(1)} %get-tuple-element.42, f32[5,64,8,64]{3,1,2,0:T(8,128)} %get-tuple-element.47, f32[5,64,8,64]{3,1,2,0:T(8,128)} %get-tuple-element.46), kind=kOutput, calls=%fused_computation.28 | convolution fusion | flops 1009579520 | bytes 9185280 | tf_op jit(solution)/shard_map/jvp(wqhd,wkhd->whqk)/dot_general | solution.py:48
  229.6 3.3 fusion.10
  233.0 1.9 multiply_reduce_fusion
  237.8 12.5 %convolution_bitcast_fusion = f32[5,256,8,128]{3,1,2,0:T(8,128)} fusion(f32[5,64,8,64]{3,1,2,0:T(8,128)S(1)} %copy-done.6, f32[5,64,8,64]{3,1,2,0:T(8,128)S(1)} %copy-done.5, f32[5,8,64,256]{3,2,1,0:T(8,128)S(1)} %get-tuple-element.57, f32[5,8,64]{2,1,0:T(8,128)S(1)} %neg.12, f32[5,8,64]{2,1,0:T(8,128)S(1)} %fusion.26, ...), kind=kOutput, calls=%fused_computation.29 | convolution fusion | flops 1010892800 | bytes 11827200 | tf_op jit(solution)/shard_map/transpose(jvp(wqhd,wkhd->whqk))/dot_general | solution.py:48
  250.3 5.7 %multiply_add_fusion.1 = (f32[5,256,8,64]{3,1,2,0:T(8,128)S(1)}, f32[5,256,8,64]{3,1,2,0:T(8,128)S(1)}) fusion(f32[5,256,8,128]{3,1,2,0:T(8,128)} %convolution_bitcast_fusion, f32[256,64]{1,0:T(8,128)} %get-tuple-element.51, f32[256,64]{1,0:T(8,128)S(1)} %get-tuple-element.50), kind=kLoop, calls=%fused_computation.14 | loop fusion | flops 4587520 | bytes 10616832 | tf_op jit(solution)/shard_map/transpose(jvp())/add_any | solution.py:38
  256.1 3.8 fusion.2
  259.9 4.7 %add_add_fusion = f32[5,256,8,128]{3,1,2,0:T(8,128)S(1)} fusion(f32[5,256,8]{1,2,0:T(8,128)S(1)} %multiply_multiply_fusion.2, f32[5,256,8]{1,2,0:T(8,128)S(1)} %fusion.35, f32[8,128]{1,0:T(8,128)S(1)} %bitcast.139, f32[5,256,8,64]{3,1,2,0:T(8,128)S(1)} %get-tuple-element.41, f32[5,256,8,64]{3,1,2,0:T(8,128)S(1)} %get-tuple-element.40, ...), kind=kLoop, calls=%fused_computation.7 | loop fusion | flops 10485760 | bytes 13193216 | tf_op jit(solution)/shard_map/transpose(jvp())/add_any | solution.py:24
  268.9 2.0 fusion.27
  270.9 4.6 %copy.159 = bf16[4,256,8,128]{3,2,1,0:T(8,128)(2,1)} copy(bf16[4,256,8,128]{1,3,2,0:T(8,128)(2,1)} %fusion.27) | data formatting | bytes 4194304 | tf_op jit(solution)/shard_map/convert_element_type | solution.py:139
  275.4 5.8 %collective-permute-done.2 = bf16[256,8,128]{2,0,1:T(8,128)(2,1)} collective-permute-done((bf16[256,8,128]{2,0,1:T(8,128)(2,1)}, bf16[256,8,128]{2,0,1:T(8,128)(2,1)}, u32[]{:S(2)}, u32[]{:S(2)}) %collective-permute-start.2) | collective-permute-done | bytes 524320 | tf_op jit(solution)/shard_map/ppermute | solution.py:20
  284.9 6.9 %fusion.15 = f32[1024,2048]{1,0:T(8,128)} fusion(bf16[2048,1024]{1,0:T(8,128)(2,1)S(1)} %copy-done.38, bf16[128,8,8,128]{3,2,1,0:T(8,128)(2,1)S(1)} %bitcast.129), kind=kOutput, calls=%fused_computation.33 | convolution fusion | flops 4294967296 | bytes 14680064 | tf_op jit(solution)/shard_map/dot_general | solution.py:147
  291.8 8.4 %fusion.3 = bf16[2048,1024]{0,1:T(8,128)(2,1)} fusion(f32[1024,2048]{1,0:T(8,128)} %fusion.15, bf16[2048,1024]{1,0:T(8,128)(2,1)S(1)} %copy-done.37, bf16[128,8,8,128]{3,2,1,0:T(8,128)(2,1)S(1)} %bitcast.128), kind=kOutput, calls=%fused_computation.17 | convolution fusion | flops 4299161600 | bytes 18874368 | tf_op jit(solution)/shard_map/dot_general | solution.py:148
  300.2 40.5 %reduce-scatter.2.cloned.1.call-done = bf16[256,1024]{0,1:T(8,128)(2,1)} async-done(((bf16[2048,1024]{0,1:T(8,128)(2,1)}), bf16[256,1024]{0,1:T(8,128)(2,1)}) %reduce-scatter.2.cloned.1.call-update) | async-done | bytes 524304 | tf_op jit(solution)/shard_map/reduce_scatter | solution.py:145
  340.7 1.9 convolution_convert_fusion
  342.6 2.0 copy.160
  344.6 7.1 %all-to-all-start.1 = ((bf16[16,2,128,256]{3,2,1,0:T(8,128)(2,1)}), bf16[16,2,128,256]{3,2,1,0:T(8,128)(2,1)S(1)}, u32[]{:S(2)}, u32[]{:S(2)}) async-start(bf16[16,2,128,256]{3,2,1,0:T(8,128)(2,1)} %copy.160), calls=%async_computation.2 | async-start | bytes 4194304 | tf_op jit(solution)/shard_map/all_to_all | solution.py:159
  351.9 8.8 %fusion.23 = f32[5,64,8,128]{3,1,2,0:T(8,128)S(1)} fusion(f32[5,256,8,64]{3,1,2,0:T(8,128)} %get-tuple-element.43, f32[5,256,8,64]{3,1,2,0:T(8,128)} %copy-done.2, f32[5,8,64,256]{3,2,1,0:T(8,128)} %copy-done.39, f32[5,8,64]{2,1,0:T(8,128)S(1)} %copy-done.32, f32[5,8,64]{2,1,0:T(8,128)S(1)} %copy-done.24, f32[5,8,64]{2,1,0:T(8,128)S(1)} %copy-done.22, ...), kind=kOutput, calls=%fused_computation.46 | convolution fusion | flops 1011875840 | bytes 11827200 | tf_op jit(solution)/shard_map/transpose(jvp(wqhd,wkhd->whqk))/dot_general | solution.py:48
  365.1 19.9 %all-to-all-done.1 = bf16[16,2,128,256]{3,2,1,0:T(8,128)(2,1)S(1)} async-done(((bf16[16,2,128,256]{3,2,1,0:T(8,128)(2,1)}), bf16[16,2,128,256]{3,2,1,0:T(8,128)(2,1)S(1)}, u32[]{:S(2)}, u32[]{:S(2)}) %all-to-all-start.1) | async-done | bytes 2097184 | tf_op jit(solution)/shard_map/all_to_all | solution.py:159
  (172 shorter events, 40.0 us)
Async XLA Ops:
  7.2 74.2 %all-gather.6.cloned.1.call-start = ((), (), s32[]{:S(2)}) async-start(), calls=%async_computation.4 | async-start | bytes 4456448 | tf_op jit(solution)/shard_map/all_gather | solution.py:69
  12.8 44.8 %copy-start.13 = (bf16[256,1024]{1,0:T(8,128)(2,1)S(1)}, bf16[256,1024]{1,0:T(8,128)(2,1)}, u32[]{:S(2)}) copy-start(bf16[256,1024]{1,0:T(8,128)(2,1)} %param.14) | copy-start | bytes 1572868
  12.8 42.4 %all-to-all-start = ((bf16[16,2,128,256]{3,2,1,0:T(8,128)(2,1)}), bf16[16,2,128,256]{3,2,1,0:T(8,128)(2,1)S(1)}, u32[]{:S(2)}, u32[]{:S(2)}) async-start(bf16[16,2,128,256]{3,2,1,0:T(8,128)(2,1)} %select_select_fusion), calls=%async_computation | async-start | bytes 4194304 | tf_op jit(solution)/shard_map/all_to_all | solution.py:86
  20.6 98.5 %all-gather.4.cloned.1.call-start = ((), (), s32[]{:S(2)}) async-start(), calls=%async_computation.3 | async-start | bytes 4718592 | tf_op jit(solution)/shard_map/all_gather | solution.py:91
  20.8 38.4 %copy-start.35 = (s32[8]{0:T(128)}, s32[8]{0:T(128)S(1)}, u32[]{:S(2)}) copy-start(s32[8]{0:T(128)S(1)} %add_reduce_fusion) | copy-start | bytes 100
  56.7 117.4 %all-gather.8.cloned.1.call-start = ((), (), s32[]{:S(2)}) async-start(), calls=%async_computation.5 | async-start | bytes 4456448 | tf_op jit(solution)/shard_map/all_gather | solution.py:68
  57.5 283.2 %reduce-scatter.2.cloned.1.call-start = ((), (), s32[]{:S(2)}) async-start(), calls=%async_computation.6 | async-start | bytes 4718592 | tf_op jit(solution)/shard_map/reduce_scatter | solution.py:145
  61.1 65.9 %copy-start.19 = (f32[5,64,8]{1,2,0:T(8,128)}, f32[5,64,8]{1,2,0:T(8,128)S(1)}, u32[]{:S(2)}) copy-start(f32[5,64,8]{1,2,0:T(8,128)S(1)} %fusion.36) | copy-start | bytes 30724
  182.1 13.7 %collective-permute-start.1 = (bf16[256,1024]{1,0:T(8,128)(2,1)S(1)}, bf16[256,1024]{1,0:T(8,128)(2,1)S(1)}, u32[]{:S(2)}, u32[]{:S(2)}) collective-permute-start(bf16[256,1024]{1,0:T(8,128)(2,1)S(1)} %slice.114), channel_id=1, source_target_pairs={{0,8},{8,16},{16,24},{24,32},{32,40},{40,48},{48,56},{56,64},{64,7... | collective-permute-start | bytes 1572872 | tf_op jit(solution)/shard_map/ppermute | solution.py:20
  185.3 21.9 %collective-permute-start = (bf16[256,1024]{1,0:T(8,128)(2,1)}, bf16[256,1024]{1,0:T(8,128)(2,1)S(1)}, u32[]{:S(2)}, u32[]{:S(2)}) collective-permute-start(bf16[256,1024]{1,0:T(8,128)(2,1)} %slice.111), channel_id=1, source_target_pairs={{0,8},{8,16},{16,24},{24,32},{32,40},{40,48},{48,56},{56,64},{64,7... | collective-permute-start | bytes 1572872 | tf_op jit(solution)/shard_map/ppermute | solution.py:20
  196.0 13.6 %copy-start.27 = (f32[1024]{0:T(1024)S(1)}, f32[1024]{0:T(1024)}, u32[]{:S(2)}) copy-start(f32[1024]{0:T(1024)} %param.19) | copy-start | bytes 12292
  216.2 11.8 %copy-start.2 = (f32[5,256,8,64]{3,1,2,0:T(8,128)}, f32[5,256,8,64]{3,1,2,0:T(8,128)S(1)}, u32[]{:S(2)}) copy-start(f32[5,256,8,64]{3,1,2,0:T(8,128)S(1)} %get-tuple-element.42) | copy-start | bytes 7864324
  228.0 9.8 %copy-start.4 = (f32[5,8,64,256]{3,2,1,0:T(8,128)}, f32[5,8,64,256]{3,2,1,0:T(8,128)S(1)}, u32[]{:S(2)}) copy-start(f32[5,8,64,256]{3,2,1,0:T(8,128)S(1)} %get-tuple-element.55) | copy-start | bytes 7864324
  228.0 9.8 %copy-start.21 = (f32[5,8,64]{2,1,0:T(8,128)}, f32[5,8,64]{2,1,0:T(8,128)S(1)}, u32[]{:S(2)}) copy-start(f32[5,8,64]{2,1,0:T(8,128)S(1)} %get-tuple-element.54) | copy-start | bytes 30724
  228.9 8.9 %copy-start.23 = (f32[5,8,64]{2,1,0:T(8,128)}, f32[5,8,64]{2,1,0:T(8,128)S(1)}, u32[]{:S(2)}) copy-start(f32[5,8,64]{2,1,0:T(8,128)S(1)} %fusion.26) | copy-start | bytes 30724
  233.0 4.8 %copy-start.5 = (f32[5,64,8,64]{3,1,2,0:T(8,128)S(1)}, f32[5,64,8,64]{3,1,2,0:T(8,128)}, u32[]{:S(2)}) copy-start(f32[5,64,8,64]{3,1,2,0:T(8,128)} %get-tuple-element.46) | copy-start | bytes 1966084
  233.0 4.8 %copy-start.6 = (f32[5,64,8,64]{3,1,2,0:T(8,128)S(1)}, f32[5,64,8,64]{3,1,2,0:T(8,128)}, u32[]{:S(2)}) copy-start(f32[5,64,8,64]{3,1,2,0:T(8,128)} %get-tuple-element.47) | copy-start | bytes 1966084
  236.5 32.4 %collective-permute-start.3 = (bf16[256,8,128]{0,2,1:T(8,128)(2,1)}, bf16[256,8,128]{0,2,1:T(8,128)(2,1)}, u32[]{:S(2)}, u32[]{:S(2)}) collective-permute-start(bf16[256,8,128]{0,2,1:T(8,128)(2,1)} %fusion.34), channel_id=1, source_target_pairs={{8,0},{16,8},{24,16},{32,24},{40,32},{48,40},{56,48},{64,56},{72,6... | collective-permute-start | bytes 1572872 | tf_op jit(solution)/shard_map/ppermute | solution.py:20
  256.1 10.8 %slice-start = ((s8[5242880]{0:T(1024)(128)(4,1)}), s8[4194304]{0:T(1024)(128)(4,1)S(1)}, s32[]{:S(2)}) async-start(s8[5242880]{0:T(1024)(128)(4,1)} %bitcast.124), calls=%async_computation.7 | async-start | bytes 8388608
  259.9 7.0 %slice-start.1 = ((s8[5242880]{0:T(1024)(128)(4,1)}), s8[1048576]{0:T(1024)(128)(4,1)S(1)}, s32[]{:S(2)}) async-start(s8[5242880]{0:T(1024)(128)(4,1)} %bitcast.124), calls=%async_computation.8 | async-start | bytes 2097152
  265.6 15.6 %collective-permute-start.2 = (bf16[256,8,128]{2,0,1:T(8,128)(2,1)}, bf16[256,8,128]{2,0,1:T(8,128)(2,1)}, u32[]{:S(2)}, u32[]{:S(2)}) collective-permute-start(bf16[256,8,128]{2,0,1:T(8,128)(2,1)} %fusion.33), channel_id=1, source_target_pairs={{8,0},{16,8},{24,16},{32,24},{40,32},{48,40},{56,48},{64,56},{72,6... | collective-permute-start | bytes 1572872 | tf_op jit(solution)/shard_map/ppermute | solution.py:20
  284.9 6.9 %copy-start.11 = (bf16[4,256,8,128]{3,2,1,0:T(8,128)(2,1)S(1)}, bf16[4,256,8,128]{3,2,1,0:T(8,128)(2,1)}, u32[]{:S(2)}) copy-start(bf16[4,256,8,128]{3,2,1,0:T(8,128)(2,1)} %copy.159) | copy-start | bytes 6291460
  284.9 6.9 %copy-start.37 = (bf16[2048,1024]{1,0:T(8,128)(2,1)S(1)}, bf16[2048,1024]{1,0:T(8,128)(2,1)}, u32[]{:S(2)}) copy-start(bf16[2048,1024]{1,0:T(8,128)(2,1)} %all-gather.6.cloned.1.call-done) | copy-start | bytes 12582916
  300.1 40.6 %copy-start.36 = (s32[8]{0:T(128)S(1)}, s32[8]{0:T(128)}, u32[]{:S(2)}) copy-start(s32[8]{0:T(128)} %copy-done.35) | copy-start | bytes 100
  344.6 7.1 %copy-start.34 = (pred[16,2]{1,0:T(8,128)(4,1)S(1)}, pred[16,2]{1,0:T(8,128)(4,1)}, u32[]{:S(2)}) copy-start(pred[16,2]{1,0:T(8,128)(4,1)} %copy-done.33) | copy-start | bytes 100
  344.6 7.2 %copy-start.26 = (s32[16,2]{1,0:T(8,128)S(1)}, s32[16,2]{1,0:T(8,128)}, u32[]{:S(2)}) copy-start(s32[16,2]{1,0:T(8,128)} %copy-done.25) | copy-start | bytes 388
  344.6 7.3 %copy-start.22 = (f32[5,8,64]{2,1,0:T(8,128)S(1)}, f32[5,8,64]{2,1,0:T(8,128)}, u32[]{:S(2)}) copy-start(f32[5,8,64]{2,1,0:T(8,128)} %copy-done.21) | copy-start | bytes 30724
  344.6 7.3 %copy-start.24 = (f32[5,8,64]{2,1,0:T(8,128)S(1)}, f32[5,8,64]{2,1,0:T(8,128)}, u32[]{:S(2)}) copy-start(f32[5,8,64]{2,1,0:T(8,128)} %copy-done.23) | copy-start | bytes 30724
  344.6 7.3 %copy-start.32 = (f32[5,8,64]{2,1,0:T(8,128)S(1)}, f32[5,8,64]{2,1,0:T(8,128)}, u32[]{:S(2)}) copy-start(f32[5,8,64]{2,1,0:T(8,128)} %copy-done.31) | copy-start | bytes 30724
  344.6 40.4 %all-to-all-start.1 = ((bf16[16,2,128,256]{3,2,1,0:T(8,128)(2,1)}), bf16[16,2,128,256]{3,2,1,0:T(8,128)(2,1)S(1)}, u32[]{:S(2)}, u32[]{:S(2)}) async-start(bf16[16,2,128,256]{3,2,1,0:T(8,128)(2,1)} %copy.160), calls=%async_computation.2 | async-start | bytes 4194304 | tf_op jit(solution)/shard_map/all_to_all | solution.py:159
  351.9 8.8 %copy-start.16 = (f32[64,64]{1,0:T(8,128)S(1)}, f32[64,64]{1,0:T(8,128)}, u32[]{:S(2)}) copy-start(f32[64,64]{1,0:T(8,128)} %copy-done.15) | copy-start | bytes 49156
  364.0 23.1 %copy-start.1 = (bf16[4,128,256]{2,1,0:T(8,128)(2,1)S(1)}, bf16[4,128,256]{2,1,0:T(8,128)(2,1)}, u32[]{:S(2)}) copy-start(bf16[4,128,256]{2,1,0:T(8,128)(2,1)} %param.15) | copy-start | bytes 786436
  (20 other events, 46.7 us)
Sparse Core Ops, SparseCore 0:
  10.2 71.1 all-gather.5
  83.6 35.3 all-gather.3
  121.2 52.8 all-gather.7
  300.3 40.3 reduce-scatter.1
where the time goes:
time: 402 us; the launch traced here: 394 us
  waiting for transfers between devices  214 us (53%)
  matrix products  72.5 us (18%)
  other arithmetic  38.2 us (10%)
  local copies, waits for them, and re-layouts  29.7 us (7%)
  starting transfers between devices  24.2 us (6%)
  between operations  14.9 us (4%)
    all_gather x1, waiting for transfers between devices, shards(): lax.all_gather(key_weight, 'ctx', axis=0, tiled=True)  45 us
    reduce_scatter x1, waiting for transfers between devices, shards(): lax.psum_scatter((lax.dot_general(key_rows, key_grad, contract, preferred...  40.5 us
    all_gather x1, waiting for transfers between devices, shards(): block_rows = lax.all_gather(received, 'enc', axis=2, tiled=True)  37.7 us
    all_to_all x1, waiting for transfers between devices, shards(): lax.all_to_all(outgoing, 'ctx', split_axis=0, concat_axis=0, tiled=True)  34.4 us
    dot_general x3, matrix products, attend(): jnp.einsum('wqhd,wkhd->whqk', query_rot, key_rot, precision=PRECISE)  33.1 us
    all_to_all x1, waiting for transfers between devices, shards(): lax.all_to_all(returning.reshape(members, CAP, NT, feature_width).astype(...  19.9 us
    all_gather x1, waiting for transfers between devices, shards(): lax.all_gather(value_weight, 'ctx', axis=0, tiled=True)  18.7 us
    ppermute x4, waiting for transfers between devices, from_behind(): lax.ppermute(value, axis, [(source, source + steps) for source in range(l...  17 us
  transfers between devices with their start and end apart: 10, of which 8 were waited for; matrix products, arithmetic and copies ran while one was open for 19% of the time, Pallas kernels for 0%

commit v1 on v0

v1 whole, which is shorter than its diff:
```python
import functools

import jax
import jax.numpy as jnp
import numpy as np
from jax import lax
from jax.experimental import pallas as pl
from jax.experimental.pallas import tpu as pltpu
from jax.sharding import PartitionSpec as P

MESH = pl.DeviceIdType.MESH
F32 = jnp.float32
BF16 = jnp.bfloat16

DH = 128
SPAN = 64
NT = 128
EPSILON = 1e-06
LOG_BASE = 9.210340371976184
SCALE = DH**-0.5
CHUNKS = 4
CW = 256

NT_DIMS = (((1,), (1,)), ((), ()))
TN_DIMS = (((0,), (0,)), ((), ()))


def rope_tables():
    half = DH // 2
    freq = np.exp(np.arange(half) * (-2.0 * LOG_BASE / DH))
    angle = np.arange(NT)[:, None] * freq[None, :]
    cos = np.concatenate([np.cos(angle)] * 2, axis=1)
    sin = np.concatenate([-np.sin(angle), np.sin(angle)], axis=1)
    twice = lambda t: np.concatenate([t, t], axis=0).astype(np.float32)
    return twice(cos), twice(sin)


def swap(v):
    return pltpu.roll(v, DH // 2, 1)


def unit(v):
    r = lax.rsqrt(jnp.mean(v * v, axis=1, keepdims=True) + EPSILON)
    return v * r, r


def rope(v, cos, sin):
    return v * cos + swap(v) * sin


def rope_back(d, cos, sin):
    return d * cos + swap(d * sin)


def unit_back(d, xhat, r):
    return r * (d - xhat * jnp.mean(d * xhat, axis=1, keepdims=True))


def kernel(
    q_ref, do_ref, pool_ref, kw_ref, vw_ref, qg_ref, kg_ref, cos_ref, sin_ref, owner_ref, slot_ref,
    qgrad_ref, sgrad_ref,
    pool_all, kw_all, vw_all, ebuf, halo_out, halo, qwin, qbd, dobd, dqwin, qback_out, qback, dkv,
    sib_out, sib_in, own, t_out, t_in, m_out, m_in, refg, ret_out, ret_in, stab,
    ag_s, ag_r, e_s, e_r, sib_s, sib_r, h_s, h_r, rs_s, rs_r, a2a_s, a2a_r,
):
    c, e = lax.axis_index("ctx"), lax.axis_index("enc")
    z, x = c // 4, c % 4
    y, core = e // 2, e % 2
    up, dn = (y + 1) % 4, (y + 3) % 4
    enc = lambda y_, core_: y_ * 2 + core_
    pending = []

    def send(src, dst, ssem, rsem, dev):
        cp = pltpu.make_async_remote_copy(
            src_ref=src, dst_ref=dst, send_sem=ssem, recv_sem=rsem, device_id=dev, device_id_type=MESH
        )
        cp.start()
        pending.append(cp)
        return cp

    barrier = pltpu.get_barrier_semaphore()
    for d in range(1, 16):
        pl.semaphore_signal(barrier, inc=1, device_id=((c + d) % 16, e), device_id_type=MESH)
    for other in (enc(up, core), enc(dn, core), enc(y, 1 - core)):
        pl.semaphore_signal(barrier, inc=1, device_id=(c, other), device_id_type=MESH)
    pl.semaphore_wait(barrier, 18)

    class Item:
        def __init__(self, n, bufs, blocks):
            self.n, self.bufs, self.blocks = n, bufs, blocks
            self.cp = {}

        def view(self, ab, first, second):
            zi, xi = (second, first) if ab == 0 else (first, second)
            ref = self.bufs[ab]
            if self.blocks[ab] is None:
                return ref.at[zi, xi]
            return ref.at[zi, xi, self.blocks[ab]]

        def half(self, ab, first, second, h):
            zi, xi = (second, first) if ab == 0 else (first, second)
            ref = self.bufs[ab]
            if self.blocks[ab] is None:
                return ref.at[zi, xi, pl.ds(64 * h, 64)]
            return ref.at[zi, xi, pl.ds(self.blocks[ab].start + h, 1)]

        def coords(self, ab):
            return (x, z) if ab == 0 else (z, x)

        def dev(self, ab, first, second):
            return (second * 4 + first, e) if ab == 0 else (first * 4 + second, e)

        def go(self, step, ab, d, ref, to):
            self.cp[step, ab, d] = send(
                ref, ref, ag_s.at[self.n, ab, step, d], ag_r.at[self.n, ab, step, d], to
            )

        def s1(self):
            for ab in (0, 1):
                f, s = self.coords(ab)
                for d in (0, 1):
                    to = self.dev(ab, (f + (1, 3)[d]) % 4, s)
                    self.go(0, ab, d, self.view(ab, f, s), to)

        def s2(self):
            for ab in (0, 1):
                f, s = self.coords(ab)
                for d in (0, 1):
                    self.cp[0, ab, d].wait_recv()
                    to = self.dev(ab, (f + (1, 3)[d]) % 4, s)
                    self.go(1, ab, d, self.half(ab, (f + (3, 1)[d]) % 4, s, d), to)

        def s3(self):
            for ab in (0, 1):
                f, s = self.coords(ab)
                for d in (0, 1):
                    self.cp[1, ab, d].wait_recv()
                for d in (0, 1):
                    to = self.dev(ab, f, (s + (1, 3)[d]) % 4)
                    self.go(2, ab, d, self.view(ab, pl.ds(0, 4), s), to)

        def s4(self):
            for ab in (0, 1):
                f, s = self.coords(ab)
                for d in (0, 1):
                    self.cp[2, ab, d].wait_recv()
                    to = self.dev(ab, f, (s + (1, 3)[d]) % 4)
                    self.go(3, ab, d, self.view(ab, pl.ds(2 * d, 2), (s + (3, 1)[d]) % 4), to)

        def done(self):
            for ab in (0, 1):
                for d in (0, 1):
                    self.cp[3, ab, d].wait_recv()

    pool = Item(0, (pool_all, pool_all), (pl.ds(0, 2), pl.ds(2, 2)))
    w = [Item(1 + j, (kw_all.at[j], vw_all.at[j]), (None, None)) for j in range(CHUNKS)]

    pool_all[z, x] = pool_ref[...]
    pool.s1()
    halo_out[0] = q_ref[0:SPAN, :]
    halo_out[1] = do_ref[0:SPAN, :]
    halo_cp = send(halo_out, halo, h_s.at[0], h_r.at[0], ((c + 15) % 16, e))
    for j in range(CHUNKS):
        kw_all[j, z, x] = kw_ref[:, j * CW : (j + 1) * CW]
        vw_all[j, z, x] = vw_ref[:, j * CW : (j + 1) * CW]
    w[0].s1()
    pool.s2()
    pool.s3()

    def table(p, _):
        first, last, count = jnp.int32(0), jnp.int32(0), jnp.int32(0)
        r_first, r_last, r_count = jnp.int32(0), jnp.int32(0), jnp.int32(0)
        for r in range(8):
            hit = owner_ref[c * 4 + r // 2, r % 2] == p
            first = jnp.where(hit & (count == 0), r, first)
            last = jnp.where(hit, r, last)
            count = count + hit.astype(jnp.int32)
            there = owner_ref[p * 4 + r // 2, r % 2] == c
            n = slot_ref[p * 4 + r // 2, r % 2]
            r_first = jnp.where(there & (r_count == 0), n, r_first)
            r_last = jnp.where(there, n, r_last)
            r_count = r_count + there.astype(jnp.int32)
        stab[0, p], stab[1, p], stab[2, p] = first, last, count
        stab[3, p] = jnp.where(r_count > 0, r_first, -1)
        stab[4, p] = jnp.where(r_count > 1, r_last, -1)
        return 0

    lax.fori_loop(0, 16, table, 0)

    halo_cp.wait_recv()
    keep = jnp.where(c == 15, 0.0, 1.0)
    first_row = lax.broadcasted_iota(jnp.int32, (4 * SPAN, DH), 0) == 0

    def windows(ref, which, cols):
        own_rows = ref[:, cols].astype(F32)
        nxt = halo[which, :, cols].astype(F32) * keep
        shifted = pltpu.roll(jnp.concatenate([own_rows[SPAN:], nxt], axis=0), 1, 0)
        return jnp.where(first_row, own_rows[SPAN - 1 : SPAN], shifted)

    qcos = jnp.concatenate([cos_ref[0:SPAN, :]] * 4, axis=0)
    qsin = jnp.concatenate([sin_ref[0:SPAN, :]] * 4, axis=0)
    zero = jnp.zeros((SPAN, DH), BF16)

    def prepare(h):
        j, hh = h // 2, h % 2
        cols = pl.ds(h * DH, DH)
        v = windows(q_ref, 0, cols)
        qwin[h] = v
        xhat, _ = unit(v)
        rot = (rope(xhat * qg_ref[:, cols], qcos, qsin) * SCALE).astype(BF16)
        dov = windows(do_ref, 1, cols).astype(BF16)
        for s in range(4):
            r = slice(s * SPAN, (s + 1) * SPAN)
            mine = slice(hh * DH, (hh + 1) * DH)
            rest = slice((1 - hh) * DH, (2 - hh) * DH)
            rows = slice(hh * SPAN, (hh + 1) * SPAN)
            qbd[j, s, rows, mine] = rot[r]
            qbd[j, s, rows, rest] = zero
            dobd[j, s, rows, mine] = dov[r]
            dobd[j, s, rows, rest] = zero

    for h in range(8):
        prepare(h)

    w[0].s2()
    w[1].s1()
    pool.s4()
    w[0].s3()
    pool.done()

    for r in range(8):
        o, n = owner_ref[c * 4 + r // 2, r % 2], slot_ref[c * 4 + r // 2, r % 2]
        ebuf[e, r * NT : (r + 1) * NT, :] = pool_all[o // 4, o % 4, n]

    ring = {}
    sib = {}
    for d, to in ((0, up), (1, dn)):
        ring[0, d] = send(ebuf.at[e], ebuf.at[e], e_s.at[0, d], e_r.at[0, d], (c, enc(to, core)))
    other = (c, enc(y, 1 - core))

    def to_sibling(i, slot):
        sib[i] = send(ebuf.at[slot], ebuf.at[slot], sib_s.at[i], sib_r.at[i], other)

    to_sibling(0, e)
    w[1].s2()
    w[2].s1()
    w[0].s4()
    w[1].s3()
    for d, frm, to in ((0, dn, up), (1, up, dn)):
        ring[0, d].wait_recv()
        slot = enc(frm, core)
        part = ebuf.at[slot, pl.ds(512 * d, 512)]
        ring[1, d] = send(part, part, e_s.at[1, d], e_r.at[1, d], (c, enc(to, core)))
        to_sibling(1 + d, slot)
    w[2].s2()
    w[3].s1()
    for d in (0, 1):
        ring[1, d].wait_recv()
    to_sibling(3, enc((y + 2) % 4, core))
    w[1].s4()
    w[2].s3()
    w[3].s2()
    for i in range(4):
        sib[i].wait_recv()

    def compute(j):
        kw = kw_all[j].reshape(2048, CW)
        vw = vw_all[j].reshape(2048, CW)

        def span(s, _):
            rows = pl.ds(pl.multiple_of(s * 256, 256), 256)
            ecat = jnp.concatenate([ebuf[i, rows, :] for i in range(8)], axis=1)
            kp = jnp.dot(ecat, kw, preferred_element_type=F32).astype(BF16).astype(F32)
            vp = jnp.dot(ecat, vw, preferred_element_type=F32).astype(BF16)
            cos, sin = cos_ref[...], sin_ref[...]
            hats, rs, gains, ks = [], [], [], []
            for hh in range(2):
                xhat, r = unit(kp[:, hh * DH : (hh + 1) * DH])
                g = kg_ref[:, (2 * j + hh) * DH : (2 * j + hh + 1) * DH]
                ks.append(rope(xhat * g, cos, sin).astype(BF16))
                hats.append(xhat)
                rs.append(r)
                gains.append(g)
            k = jnp.concatenate(ks, axis=1)
            qb, dob = qbd[j, s], dobd[j, s]
            scores = lax.dot_general(k, qb, NT_DIMS, preferred_element_type=F32)
            dp = lax.dot_general(vp, dob, NT_DIMS, preferred_element_type=F32)
            p = jnp.exp(scores)
            p = p * (1.0 / jnp.sum(p, axis=0, keepdims=True))
            ds = (p * (dp - jnp.sum(p * dp, axis=0, keepdims=True))).astype(BF16)
            dv = jnp.dot(p.astype(BF16), dob, preferred_element_type=F32)
            dk = jnp.dot(ds, qb, preferred_element_type=F32)
            dq = lax.dot_general(ds, k, TN_DIMS, preferred_element_type=F32) * SCALE
            base = j * 512
            for hh in range(2):
                cols = slice(hh * DH, (hh + 1) * DH)
                d = rope_back(dk[:, cols], cos, sin) * gains[hh]
                dkv[rows, base + hh * DH : base + (hh + 1) * DH] = unit_back(d, hats[hh], rs[hh]).astype(BF16)
            dkv[rows, base + 256 : base + 512] = dv.astype(BF16)
            qrows = pl.ds(pl.multiple_of(s * SPAN, SPAN), SPAN)
            for hh in range(2):
                h = 2 * j + hh
                xhat, r = unit(qwin[h, qrows, :])
                d = dq[hh * SPAN : (hh + 1) * SPAN, hh * DH : (hh + 1) * DH]
                d = rope_back(d, cos_ref[0:SPAN, :], sin_ref[0:SPAN, :]) * qg_ref[:, h * DH : (h + 1) * DH]
                dqwin[qrows, h * DH : (h + 1) * DH] = unit_back(d, xhat, r)
            return 0

        lax.fori_loop(0, 4, span, 0)

    w[0].done()
    compute(0)
    w[2].s4()
    w[3].s3()
    w[1].done()
    compute(1)
    w[3].s4()
    w[2].done()
    compute(2)
    w[3].done()
    compute(3)

    def shifted_back(cols):
        return pltpu.roll(dqwin[:, cols], 4 * SPAN - 1, 0)

    for h in range(8):
        cols = slice(h * DH, (h + 1) * DH)
        back = shifted_back(cols).astype(BF16)
        qgrad_ref[SPAN:, cols] = back[: 3 * SPAN]
        qback_out[:, cols] = back[3 * SPAN :]
    qback_cp = send(qback_out, qback, h_s.at[1], h_r.at[1], ((c + 1) % 16, e))

    rs_cp = {}

    def product(f, which, out):
        xi = 2 * which + f
        wcat = jnp.concatenate(
            [b[j, :, xi].reshape(512, CW) for j in range(CHUNKS) for b in (kw_all, vw_all)], axis=1
        )

        def span(s, _):
            rows = pl.ds(pl.multiple_of(s * 256, 256), 256)
            part = lax.dot_general(dkv[rows, :], wcat, NT_DIMS, preferred_element_type=F32)
            for i in range(4):
                out[f, i, rows, :] = part[:, i * 128 : (i + 1) * 128].astype(out.dtype)
            return 0

        lax.fori_loop(0, 4, span, 0)

    def rs_a(f):
        product(f, 1 - core, sib_out)
        rs_cp[f, 0] = send(sib_out.at[f], sib_in.at[f], rs_s.at[f, 0], rs_r.at[f, 0], other)
        product(f, core, own)

    def rs_b(f):
        rs_cp[f, 0].wait_recv()
        opp = (y + 2) % 4
        for d, to in ((0, up), (1, dn)):
            rows = slice(512 * d, 512 * d + 512)
            t_out[f, d] = (own[f, opp, rows, :] + sib_in[f, opp, rows, :].astype(F32)).astype(BF16)
            rs_cp[f, 1, d] = send(
                t_out.at[f, d], t_in.at[f, d], rs_s.at[f, 1 + d], rs_r.at[f, 1 + d], (c, enc(to, core))
            )

    def rs_c(f):
        for d, to in ((0, up), (1, dn)):
            rs_cp[f, 1, d].wait_recv()
            rows = slice(512 * d, 512 * d + 512)
            rest = slice(512 - 512 * d, 1024 - 512 * d)
            both = lambda r: own[f, to, r, :] + sib_in[f, to, r, :].astype(F32)
            m_out[f, d, rows, :] = (both(rows) + t_in[f, d].astype(F32)).astype(BF16)
            m_out[f, d, rest, :] = both(rest).astype(BF16)
            rs_cp[f, 2, d] = send(
                m_out.at[f, d], m_in.at[f, d], rs_s.at[f, 3 + d], rs_r.at[f, 3 + d], (c, enc(to, core))
            )

    def rs_d(f):
        for d in (0, 1):
            rs_cp[f, 2, d].wait_recv()
        for r in range(8):
            rows = slice(r * NT, (r + 1) * NT)
            refg[f, r] = (
                own[f, y, rows, :]
                + sib_in[f, y, rows, :].astype(F32)
                + m_in[f, 0, rows, :].astype(F32)
                + m_in[f, 1, rows, :].astype(F32)
            )
        for d in range(16):
            p = (c + d) % 16
            count = stab[2, p]
            one = jnp.where(count > 0, 1.0, 0.0)
            two = jnp.where(count > 1, 1.0, 0.0)
            block0 = (refg[f, stab[0, p]] * one).astype(BF16)
            block1 = (refg[f, stab[1, p]] * two).astype(BF16)
            if d == 0:
                ret_in[f, c, 0] = block0
                ret_in[f, c, 1] = block1
                continue
            ret_out[f, d, 0] = block0
            ret_out[f, d, 1] = block1
            rs_cp[f, 3, d] = send(
                ret_out.at[f, d], ret_in.at[f, c], a2a_s.at[f, d], a2a_r.at[f, d], (p, e)
            )

    def rs_e(f):
        for d in range(1, 16):
            rs_cp[f, 3, d].wait_recv()

        def add(p, accs):
            b0, b1 = ret_in[f, p, 0].astype(F32), ret_in[f, p, 1].astype(F32)
            n0, n1 = stab[3, p], stab[4, p]
            return tuple(
                a + b0 * jnp.where(n0 == n, 1.0, 0.0) + b1 * jnp.where(n1 == n, 1.0, 0.0)
                for n, a in enumerate(accs)
            )

        for n, a in enumerate(lax.fori_loop(0, 16, add, tuple(jnp.zeros((NT, 128), F32) for _ in range(4)))):
            sgrad_ref[n, :, f * 128 : (f + 1) * 128] = a

    rs_a(0)
    rs_b(0)
    rs_a(1)
    rs_c(0)
    rs_b(1)
    rs_d(0)
    rs_c(1)
    rs_e(0)
    rs_d(1)

    qback_cp.wait_recv()
    live = jnp.where(c == 0, 0.0, 1.0)
    last_row = lax.broadcasted_iota(jnp.int32, (SPAN, DH), 0) == SPAN - 1
    for h in range(8):
        cols = slice(h * DH, (h + 1) * DH)
        head = qback[:, cols].astype(F32) * live
        qgrad_ref[0:SPAN, cols] = jnp.where(last_row, dqwin[0:1, cols], head).astype(BF16)

    rs_e(1)
    for cp in pending:
        cp.wait_send()


def shards(queries, out_grad, nbr_states, key_weight, value_weight, q_gain, k_gain, nbr_owner, nbr_slot):
    cos, sin = rope_tables()
    vmem = pl.BlockSpec(memory_space=pltpu.VMEM)
    smem = pl.BlockSpec(memory_space=pltpu.SMEM)
    dma = pltpu.SemaphoreType.DMA
    return pl.pallas_call(
        kernel,
        out_shape=(
            jax.ShapeDtypeStruct((256, 1024), BF16),
            jax.ShapeDtypeStruct((4, NT, 256), F32),
        ),
        in_specs=[vmem] * 9 + [smem] * 2,
        out_specs=(vmem, vmem),
        scratch_shapes=[
            pltpu.VMEM((4, 4, 4, NT, 256), BF16),
            pltpu.VMEM((CHUNKS, 4, 4, 128, CW), BF16),
            pltpu.VMEM((CHUNKS, 4, 4, 128, CW), BF16),
            pltpu.VMEM((8, 1024, 256), BF16),
            pltpu.VMEM((2, SPAN, 1024), BF16),
            pltpu.VMEM((2, SPAN, 1024), BF16),
            pltpu.VMEM((8, 4 * SPAN, DH), F32),
            pltpu.VMEM((4, 4, 2 * SPAN, 256), BF16),
            pltpu.VMEM((4, 4, 2 * SPAN, 256), BF16),
            pltpu.VMEM((4 * SPAN, 1024), F32),
            pltpu.VMEM((SPAN, 1024), BF16),
            pltpu.VMEM((SPAN, 1024), BF16),
            pltpu.VMEM((1024, 2048), BF16),
            pltpu.VMEM((2, 4, 1024, 128), BF16),
            pltpu.VMEM((2, 4, 1024, 128), BF16),
            pltpu.VMEM((2, 4, 1024, 128), F32),
            pltpu.VMEM((2, 2, 512, 128), BF16),
            pltpu.VMEM((2, 2, 512, 128), BF16),
            pltpu.VMEM((2, 2, 1024, 128), BF16),
            pltpu.VMEM((2, 2, 1024, 128), BF16),
            pltpu.VMEM((2, 8, NT, 128), F32),
            pltpu.VMEM((2, 16, 2, NT, 128), BF16),
            pltpu.VMEM((2, 16, 2, NT, 128), BF16),
            pltpu.SMEM((5, 16), jnp.int32),
            dma((1 + CHUNKS, 2, 4, 2)),
            dma((1 + CHUNKS, 2, 4, 2)),
            dma((2, 2)),
            dma((2, 2)),
            dma((4,)),
            dma((4,)),
            dma((2,)),
            dma((2,)),
            dma((2, 5)),
            dma((2, 5)),
            dma((2, 16)),
            dma((2, 16)),
        ],
        compiler_params=pltpu.CompilerParams(
            collective_id=0, has_side_effects=True, vmem_limit_bytes=60 * 2**20
        ),
    )(
        queries, out_grad, nbr_states, key_weight, value_weight,
        q_gain.reshape(1, -1), k_gain.reshape(1, -1), jnp.asarray(cos), jnp.asarray(sin),
        nbr_owner, nbr_slot,
    )


def solution(mesh):
    in_specs = (
        P("ctx", "enc"),
        P("ctx", "enc"),
        P("ctx", None, "enc"),
        P("ctx", "enc"),
        P("ctx", "enc"),
        P("enc"),
        P("enc"),
        P(),
        P(),
    )
    out_specs = (P("ctx", "enc"), P("ctx", None, "enc"))
    return jax.shard_map(shards, mesh=mesh, in_specs=in_specs, out_specs=out_specs, check_vma=False)
```

time: 402 us -> 155 us (0.39)
  the two profiles are of different devices: /device:TPU:25 before, /device:TPU:1 now
where the time goes in v1:
time: 155 us; the launch traced here: 154 us
  Pallas kernels  149 us (96%)
  local copies, waits for them, and re-layouts  4.82 us (3%)
    pallas_call x1, Pallas kernels, shards(): pl.pallas_call(kernel, out_shape=(jax.ShapeDtypeStruct((256, 1024), BF16)...  149 us
    unnamed x10, local copies, waits for them, and re-layouts  4.82 us

profile of v1, /device:TPU:1, one launch (start us, length us, event | category | flops | bytes accessed | tf_op | source)
XLA Modules:
  0.0 154.4 jit_solution(13239035659993502232)
XLA Ops:
  0.6 0.0 copy-start.1
  0.6 0.7 copy-done.1
  1.3 0.0 copy-start.2
  1.3 0.7 copy.13.owner_ref
  2.0 0.0 copy-done.2
  2.0 0.7 copy.14.slot_ref
  2.7 148.9 %shard_map.122 = (bf16[256,1024]{1,0:T(8,128)(2,1)}, f32[4,128,256]{2,1,0:T(8,128)}) custom-call(bf16[256,1024]{1,0:T(8,128)(2,1)} %q_ref.1, bf16[256,1024]{1,0:T(8,128)(2,1)} %do_ref.1, bf16[4,128,256]{2,1,0:T(8,128)(2,1)} %pool_ref.1, bf16[128,1024]{1,0:T(8,128)(2,1)} %kw_ref.1, bf16[128,1024]{1,0:T(8,128)(2,1)} %vw_ref.1, f32[1,1024]{1,0:T(1,128)} %bitcast.2, ...), custom_call_target="tpu_custom_call" | custom-call | tf_op jit(solution)/shard_map/pallas_call | solution.py:448
  151.6 0.0 copy-start
  151.7 1.9 %copy.17 = bf16[256,1024]{1,0:T(8,128)(2,1)} copy(bf16[256,1024]{1,0:T(8,128)(2,1)} %get-tuple-element.4) | data formatting | bytes 1048576
  153.6 0.0 copy-done
  153.6 0.8 copy.18
Async XLA Ops:
  0.6 0.7 copy-start.1
  1.3 0.7 copy-start.2
  151.6 1.9 %copy-start = (f32[4,128,256]{2,1,0:T(8,128)S(1)}, f32[4,128,256]{2,1,0:T(8,128)}, u32[]{:S(2)}) copy-start(f32[4,128,256]{2,1,0:T(8,128)} %get-tuple-element.5) | copy-start | bytes 1572868

commit v2 on v1

v2 whole, which is shorter than its diff:
```python
import functools

import jax
import jax.numpy as jnp
import numpy as np
from jax import lax
from jax.experimental import pallas as pl
from jax.experimental.pallas import tpu as pltpu
from jax.sharding import PartitionSpec as P

MESH = pl.DeviceIdType.MESH
F32 = jnp.float32
BF16 = jnp.bfloat16

DH = 128
SPAN = 64
NT = 128
EPSILON = 1e-06
LOG_BASE = 9.210340371976184
SCALE = DH**-0.5
CHUNKS = 4
CW = 256

NT_DIMS = (((1,), (1,)), ((), ()))
TN_DIMS = (((0,), (0,)), ((), ()))


def rope_tables():
    half = DH // 2
    freq = np.exp(np.arange(half) * (-2.0 * LOG_BASE / DH))
    angle = np.arange(NT)[:, None] * freq[None, :]
    cos = np.concatenate([np.cos(angle)] * 2, axis=1)
    sin = np.concatenate([-np.sin(angle), np.sin(angle)], axis=1)
    twice = lambda t: np.concatenate([t, t], axis=0).astype(np.float32)
    return twice(cos), twice(sin)


def swap(v):
    return pltpu.roll(v, DH // 2, 1)


def unit(v):
    r = lax.rsqrt(jnp.mean(v * v, axis=1, keepdims=True) + EPSILON)
    return v * r, r


def rope(v, cos, sin):
    return v * cos + swap(v) * sin


def rope_back(d, cos, sin):
    return d * cos + swap(d * sin)


def unit_back(d, xhat, r):
    return r * (d - xhat * jnp.mean(d * xhat, axis=1, keepdims=True))


def kernel(
    q_hbm, do_hbm, pool_hbm, kw_hbm, vw_hbm, qg_hbm, kg_hbm, cos_hbm, sin_hbm, owner_ref, slot_ref,
    qgrad_hbm, sgrad_hbm,
    q_ref, do_ref, qg_ref, kg_ref, cos_ref, sin_ref, qgrad_ref, sgrad_ref,
    pool_lo, pool_hi, kw_all, vw_all, ebuf, halo, qwin, qbd, dobd, dqwin, qback_out, qback, dkv, kps, vps,
    acc, sib_out, sib_in, t_out, t_in, m_out, m_in, refg, ret_out, ret_in, stab,
    in_s, out_s, ag_s, ag_r, e_s, e_r, sib_s, sib_r, h_s, h_r, rs_s, rs_r, a2a_s, a2a_r,
):
    c, e = lax.axis_index("ctx"), lax.axis_index("enc")
    z, x = c // 4, c % 4
    y, core = e // 2, e % 2
    up, dn, opp = (y + 1) % 4, (y + 3) % 4, (y + 2) % 4
    enc = lambda y_, core_: y_ * 2 + core_
    other = (c, enc(y, 1 - core))
    pool_all = (pool_lo, pool_hi)
    pending = []

    def send(src, dst, ssem, rsem, dev):
        cp = pltpu.make_async_remote_copy(
            src_ref=src, dst_ref=dst, send_sem=ssem, recv_sem=rsem, device_id=dev, device_id_type=MESH
        )
        cp.start()
        pending.append(cp)
        return cp

    loads = []

    def load(src, dst):
        cp = pltpu.make_async_copy(src, dst, in_s.at[len(loads)])
        cp.start()
        loads.append(cp)
        return cp

    in_pool = [load(pool_hbm.at[:, :, pl.ds(128 * f, 128)], pool_all[f].at[z, x]) for f in range(2)]
    in_q = [load(q_hbm, q_ref), load(do_hbm, do_ref)]
    in_w = [
        [load(src.at[:, pl.ds(j * CW, CW)], dst.at[j, z, x]) for src, dst in ((kw_hbm, kw_all), (vw_hbm, vw_all))]
        for j in range(CHUNKS)
    ]
    in_small = [
        load(src, dst) for src, dst in ((qg_hbm, qg_ref), (kg_hbm, kg_ref), (cos_hbm, cos_ref), (sin_hbm, sin_ref))
    ]

    barrier = pltpu.get_barrier_semaphore()
    for d in range(1, 16):
        pl.semaphore_signal(barrier, inc=1, device_id=((c + d) % 16, e), device_id_type=MESH)
    for there in (enc(up, core), enc(dn, core), enc(y, 1 - core)):
        pl.semaphore_signal(barrier, inc=1, device_id=(c, there), device_id_type=MESH)
    pl.semaphore_wait(barrier, 18)

    class Item:
        def __init__(self, n, bufs, blocks=None):
            self.n, self.bufs, self.blocks = n, bufs, blocks
            self.cp = {}

        def view(self, ab, first, second):
            zi, xi = (second, first) if ab == 0 else (first, second)
            ref = self.bufs[ab]
            return ref.at[zi, xi] if self.blocks is None else ref.at[zi, xi, self.blocks[ab]]

        def half(self, ab, first, second, h):
            zi, xi = (second, first) if ab == 0 else (first, second)
            part = pl.ds(64 * h, 64) if self.blocks is None else pl.ds(self.blocks[ab].start + h, 1)
            return self.bufs[ab].at[zi, xi, part]

        def coords(self, ab):
            return (x, z) if ab == 0 else (z, x)

        def dev(self, ab, first, second):
            return (second * 4 + first, e) if ab == 0 else (first * 4 + second, e)

        def go(self, step, ab, d, ref, to):
            self.cp[step, ab, d] = send(
                ref, ref, ag_s.at[self.n, ab, step, d], ag_r.at[self.n, ab, step, d], to
            )

        def s1(self):
            for ab in (0, 1):
                f, s = self.coords(ab)
                for d in (0, 1):
                    self.go(0, ab, d, self.view(ab, f, s), self.dev(ab, (f + (1, 3)[d]) % 4, s))

        def s2(self):
            for ab in (0, 1):
                f, s = self.coords(ab)
                for d in (0, 1):
                    self.cp[0, ab, d].wait_recv()
                    to = self.dev(ab, (f + (1, 3)[d]) % 4, s)
                    self.go(1, ab, d, self.half(ab, (f + (3, 1)[d]) % 4, s, d), to)

        def s3(self):
            for ab in (0, 1):
                f, s = self.coords(ab)
                for d in (0, 1):
                    self.cp[1, ab, d].wait_recv()
                for d in (0, 1):
                    to = self.dev(ab, f, (s + (1, 3)[d]) % 4)
                    self.go(2, ab, d, self.view(ab, pl.ds(0, 4), s), to)

        def s4(self):
            for ab in (0, 1):
                f, s = self.coords(ab)
                for d in (0, 1):
                    self.cp[2, ab, d].wait_recv()
                    to = self.dev(ab, f, (s + (1, 3)[d]) % 4)
                    self.go(3, ab, d, self.view(ab, pl.ds(2 * d, 2), (s + (3, 1)[d]) % 4), to)

        def done(self):
            for ab in (0, 1):
                for d in (0, 1):
                    self.cp[3, ab, d].wait_recv()

    stored = (pl.ds(0, 2), pl.ds(2, 2))
    pool = [Item(f, (pool_all[f], pool_all[f]), stored) for f in range(2)]
    w = [Item(2 + j, (kw_all.at[j], vw_all.at[j])) for j in range(CHUNKS)]

    for f in range(2):
        in_pool[f].wait()
        pool[f].s1()
    for cp in in_w[0]:
        cp.wait()
    w[0].s1()
    for cp in in_q:
        cp.wait()
    halo_cps = [
        send(src.at[pl.ds(0, SPAN)], halo.at[i], h_s.at[i], h_r.at[i], ((c + 15) % 16, e))
        for i, src in enumerate((q_ref, do_ref))
    ]
    pool[0].s2()
    for pair in in_w[1:]:
        for cp in pair:
            cp.wait()
    w[2].s1()
    pool[1].s2()
    pool[0].s3()
    pool[1].s3()
    w[3].s1()
    w[0].s2()
    w[1].s1()
    for cp in in_small:
        cp.wait()

    def table(p, _):
        first, last, count = jnp.int32(0), jnp.int32(0), jnp.int32(0)
        r_first, r_last, r_count = jnp.int32(0), jnp.int32(0), jnp.int32(0)
        for r in range(8):
            hit = owner_ref[r % 2, c * 4 + r // 2] == p
            first = jnp.where(hit & (count == 0), r, first)
            last = jnp.where(hit, r, last)
            count = count + hit.astype(jnp.int32)
            there = owner_ref[r % 2, p * 4 + r // 2] == c
            n = slot_ref[r % 2, p * 4 + r // 2]
            r_first = jnp.where(there & (r_count == 0), n, r_first)
            r_last = jnp.where(there, n, r_last)
            r_count = r_count + there.astype(jnp.int32)
        stab[0, p], stab[1, p], stab[2, p] = first, last, count
        stab[3, p] = jnp.where(r_count > 0, r_first, -1)
        stab[4, p] = jnp.where(r_count > 1, r_last, -1)
        return 0

    lax.fori_loop(0, 16, table, 0)

    for cp in halo_cps:
        cp.wait_recv()
    keep = jnp.where(c == 15, 0.0, 1.0)
    first_row = lax.broadcasted_iota(jnp.int32, (4 * SPAN, DH), 0) == 0

    def windows(ref, which, cols):
        own_rows = ref[:, cols].astype(F32)
        nxt = halo[which, :, cols].astype(F32) * keep
        shifted = pltpu.roll(jnp.concatenate([own_rows[SPAN:], nxt], axis=0), 1, 0)
        return jnp.where(first_row, own_rows[SPAN - 1 : SPAN], shifted)

    qcos = jnp.concatenate([cos_ref[0:SPAN, :]] * 4, axis=0)
    qsin = jnp.concatenate([sin_ref[0:SPAN, :]] * 4, axis=0)
    zero = jnp.zeros((SPAN, DH), BF16)

    def prepare(h):
        j, hh = h // 2, h % 2
        cols = pl.ds(h * DH, DH)
        v = windows(q_ref, 0, cols)
        qwin[h] = v
        xhat, _ = unit(v)
        rot = (rope(xhat * qg_ref[:, cols], qcos, qsin) * SCALE).astype(BF16)
        dov = windows(do_ref, 1, cols).astype(BF16)
        for s in range(4):
            r = slice(s * SPAN, (s + 1) * SPAN)
            mine = slice(hh * DH, (hh + 1) * DH)
            rest = slice((1 - hh) * DH, (2 - hh) * DH)
            rows = slice(hh * SPAN, (hh + 1) * SPAN)
            qbd[j, s, rows, mine] = rot[r]
            qbd[j, s, rows, rest] = zero
            dobd[j, s, rows, mine] = dov[r]
            dobd[j, s, rows, rest] = zero

    for h in range(8):
        prepare(h)
    pool[0].s4()

    ring, sib = {}, {}

    def to_sibling(f, i, slot):
        ref = ebuf.at[f, slot]
        sib[f, i] = send(ref, ref, sib_s.at[f, i], sib_r.at[f, i], other)

    def y1(f):
        for r in range(8):
            o, n = owner_ref[r % 2, c * 4 + r // 2], slot_ref[r % 2, c * 4 + r // 2]
            ebuf[f, e, r * NT : (r + 1) * NT, :] = pool_all[f][o // 4, o % 4, n]
        for d, to in ((0, up), (1, dn)):
            ref = ebuf.at[f, e]
            ring[f, 0, d] = send(ref, ref, e_s.at[f, 0, d], e_r.at[f, 0, d], (c, enc(to, core)))
        to_sibling(f, 0, e)

    def y2(f):
        for d, frm, to in ((0, dn, up), (1, up, dn)):
            ring[f, 0, d].wait_recv()
            slot = enc(frm, core)
            part = ebuf.at[f, slot, pl.ds(512 * d, 512)]
            ring[f, 1, d] = send(part, part, e_s.at[f, 1, d], e_r.at[f, 1, d], (c, enc(to, core)))
            to_sibling(f, 1 + d, slot)

    def y3(f):
        for d in (0, 1):
            ring[f, 1, d].wait_recv()
        to_sibling(f, 3, enc(opp, core))

    pool[1].s4()
    w[0].s3()
    pool[0].done()
    y1(0)
    w[1].s2()
    w[3].s2()
    w[2].s2()
    pool[1].done()
    y1(1)
    w[0].s4()
    w[1].s3()
    y2(0)
    w[2].s3()
    y2(1)
    y3(0)
    y3(1)
    w[0].done()
    for f in range(2):
        for i in range(4):
            sib[f, i].wait_recv()

    def project(j, s):
        rows = slice(s * 256, (s + 1) * 256)
        ecat = jnp.concatenate([ebuf[f, i, rows, :] for i in range(8) for f in range(2)], axis=1)
        kw, vw = kw_all[j].reshape(2048, CW), vw_all[j].reshape(2048, CW)
        kps[s % 2] = jnp.dot(ecat, kw, preferred_element_type=F32).astype(BF16).astype(F32)
        vps[s % 2] = jnp.dot(ecat, vw, preferred_element_type=F32).astype(BF16)

    def keep_rows(s, cols, v):
        for rr in range(2):
            for h in range(2):
                to = h * 512 + (2 * s + rr) * 64
                dkv[to : to + 64, cols] = v[rr * NT + h * 64 : rr * NT + h * 64 + 64]

    def attend(j, s):
        rows = slice(s * 256, (s + 1) * 256)
        kp, vp = kps[s % 2], vps[s % 2]
        cos, sin = cos_ref[...], sin_ref[...]
        hats, rs, gains, ks = [], [], [], []
        for hh in range(2):
            xhat, r = unit(kp[:, hh * DH : (hh + 1) * DH])
            g = kg_ref[:, (2 * j + hh) * DH : (2 * j + hh + 1) * DH]
            ks.append(rope(xhat * g, cos, sin).astype(BF16))
            hats.append(xhat)
            rs.append(r)
            gains.append(g)
        k = jnp.concatenate(ks, axis=1)
        qb, dob = qbd[j, s], dobd[j, s]
        scores = lax.dot_general(k, qb, NT_DIMS, preferred_element_type=F32)
        dp = lax.dot_general(vp, dob, NT_DIMS, preferred_element_type=F32)
        p = jnp.exp(scores)
        p = p * (1.0 / jnp.sum(p, axis=0, keepdims=True))
        ds = (p * (dp - jnp.sum(p * dp, axis=0, keepdims=True))).astype(BF16)
        dv = jnp.dot(p.astype(BF16), dob, preferred_element_type=F32)
        dk = jnp.dot(ds, qb, preferred_element_type=F32)
        dq = lax.dot_general(ds, k, TN_DIMS, preferred_element_type=F32) * SCALE
        for hh in range(2):
            cols = slice(hh * DH, (hh + 1) * DH)
            d = rope_back(dk[:, cols], cos, sin) * gains[hh]
            keep_rows(s, cols, unit_back(d, hats[hh], rs[hh]).astype(BF16))
        keep_rows(s, slice(CW, 2 * CW), dv.astype(BF16))
        qrows = slice(s * SPAN, (s + 1) * SPAN)
        for hh in range(2):
            h = 2 * j + hh
            xhat, r = unit(qwin[h, qrows, :])
            d = dq[hh * SPAN : (hh + 1) * SPAN, hh * DH : (hh + 1) * DH]
            d = rope_back(d, cos_ref[0:SPAN, :], sin_ref[0:SPAN, :]) * qg_ref[:, h * DH : (h + 1) * DH]
            dqwin[qrows, h * DH : (h + 1) * DH] = unit_back(d, xhat, r)

    def compute(j, part):
        if part == 0:
            project(j, 0)
        for s in (2 * part, 2 * part + 1):
            if s < 3:
                project(j, s + 1)
            attend(j, s)

    def product(j, f, which):
        xi = 2 * (core if which else 1 - core) + f
        for i in range(2):
            wcat = jnp.concatenate([b[j, 2 * i : 2 * i + 2, xi].reshape(256, CW) for b in (kw_all, vw_all)], axis=1)
            part = lax.dot_general(dkv[...], wcat, NT_DIMS, preferred_element_type=F32)
            for k in range(2):
                new = part[:, k * 128 : (k + 1) * 128]
                if j > 0:
                    new = new + acc[f, which, 2 * i + k]
                if j == CHUNKS - 1 and which == 0:
                    sib_out[f, 2 * i + k] = new.astype(BF16)
                else:
                    acc[f, which, 2 * i + k] = new

    def products(j):
        for f in range(2):
            for which in range(2):
                product(j, f, which)

    def query_rows(j):
        for h in (2 * j, 2 * j + 1):
            cols = slice(h * DH, (h + 1) * DH)
            back = pltpu.roll(dqwin[:, cols], 4 * SPAN - 1, 0).astype(BF16)
            qgrad_ref[SPAN:, cols] = back[: 3 * SPAN]
            qback_out[:, cols] = back[3 * SPAN :]

    compute(0, 0)
    w[1].s4()
    compute(0, 1)
    w[2].s4()
    products(0)
    w[3].s3()
    w[1].done()
    compute(1, 0)
    compute(1, 1)
    products(1)
    query_rows(0)
    query_rows(1)
    w[2].done()
    compute(2, 0)
    w[3].s4()
    compute(2, 1)
    products(2)
    query_rows(2)
    w[3].done()
    compute(3, 0)
    compute(3, 1)

    rs_cp = {}

    def rs_send(p, k, src, dst, to):
        rs_cp[p, k] = send(src, dst, rs_s.at[p, k], rs_r.at[p, k], to)

    def rs_a(f):
        product(CHUNKS - 1, f, 0)
        for h in range(2):
            rows = pl.ds(512 * h, 512)
            rs_send(2 * f + h, 0, sib_out.at[f, :, rows], sib_in.at[f, :, rows], other)
        product(CHUNKS - 1, f, 1)

    def both(p, i, start, size):
        rows = pl.ds(512 * (p % 2) + start, size)
        return acc[p // 2, 1, i, rows, :] + sib_in[p // 2, i, rows, :].astype(F32)

    sides = ((0, up), (1, dn))

    def rs_b(p):
        rs_cp[p, 0].wait_recv()
        for d, to in sides:
            t_out[p, d] = both(p, opp, 256 * d, 256).astype(BF16)
            rs_send(p, 1 + d, t_out.at[p, d], t_in.at[p, d], (c, enc(to, core)))
        for d, to in sides:
            m_out[p, d, 1 - d] = both(p, to, 256 * (1 - d), 256).astype(BF16)
            rs_send(p, 3 + d, m_out.at[p, d, 1 - d], m_in.at[p, d, 1 - d], (c, enc(to, core)))

    def rs_c(p):
        for d, to in sides:
            mine = both(p, to, 256 * d, 256)
            rs_cp[p, 1 + d].wait_recv()
            m_out[p, d, d] = (mine + t_in[p, d].astype(F32)).astype(BF16)
            rs_send(p, 5 + d, m_out.at[p, d, d], m_in.at[p, d, d], (c, enc(to, core)))

    def rs_d(p):
        for k in range(3, 7):
            rs_cp[p, k].wait_recv()
        for h in range(2):
            total = both(p, y, 256 * h, 256) + m_in[p, 0, h].astype(F32) + m_in[p, 1, h].astype(F32)
            refg[p, 4 * h : 4 * h + 4] = total.reshape(4, 64, 128)
        for d in range(16):
            to = (c + d) % 16
            count = stab[2, to]
            one = jnp.where(count > 0, 1.0, 0.0)
            two = jnp.where(count > 1, 1.0, 0.0)
            block0 = (refg[p, stab[0, to]] * one).astype(BF16)
            block1 = (refg[p, stab[1, to]] * two).astype(BF16)
            if d == 0:
                ret_in[p, c, 0] = block0
                ret_in[p, c, 1] = block1
                continue
            ret_out[p, d, 0] = block0
            ret_out[p, d, 1] = block1
            rs_cp[p, 7, d] = send(
                ret_out.at[p, d], ret_in.at[p, c], a2a_s.at[p, d], a2a_r.at[p, d], (to, e)
            )

    outs = []

    def store(src, dst):
        cp = pltpu.make_async_copy(src, dst, out_s.at[len(outs)])
        cp.start()
        outs.append(cp)

    def rs_e(p):
        for d in range(1, 16):
            rs_cp[p, 7, d].wait_recv()

        def add(o, sums):
            b0, b1 = ret_in[p, o, 0].astype(F32), ret_in[p, o, 1].astype(F32)
            n0, n1 = stab[3, o], stab[4, o]
            return tuple(
                a + b0 * jnp.where(n0 == n, 1.0, 0.0) + b1 * jnp.where(n1 == n, 1.0, 0.0)
                for n, a in enumerate(sums)
            )

        for n, a in enumerate(lax.fori_loop(0, 16, add, tuple(jnp.zeros((64, 128), F32) for _ in range(4)))):
            sgrad_ref[p, n] = a
        store(sgrad_ref.at[p], sgrad_hbm.at[:, pl.ds(64 * (p % 2), 64), pl.ds(128 * (p // 2), 128)])

    rs_a(0)
    rs_b(0)
    query_rows(3)
    qback_cp = send(qback_out, qback, h_s.at[2], h_r.at[2], ((c + 1) % 16, e))
    rs_c(0)
    rs_b(1)
    rs_d(0)
    rs_c(1)
    rs_a(1)
    rs_d(1)
    rs_b(2)
    rs_c(2)
    rs_b(3)
    store(qgrad_ref.at[pl.ds(SPAN, 3 * SPAN)], qgrad_hbm.at[pl.ds(SPAN, 3 * SPAN)])
    rs_d(2)
    rs_c(3)
    rs_d(3)

    qback_cp.wait_recv()
    live = jnp.where(c == 0, 0.0, 1.0)
    last_row = lax.broadcasted_iota(jnp.int32, (SPAN, DH), 0) == SPAN - 1
    for h in range(8):
        cols = slice(h * DH, (h + 1) * DH)
        head = qback[:, cols].astype(F32) * live
        qgrad_ref[0:SPAN, cols] = jnp.where(last_row, dqwin[0:1, cols], head).astype(BF16)
    store(qgrad_ref.at[pl.ds(0, SPAN)], qgrad_hbm.at[pl.ds(0, SPAN)])

    for p in range(4):
        rs_e(p)
    for cp in outs:
        cp.wait()
    for cp in pending:
        cp.wait_send()


def shards(queries, out_grad, nbr_states, key_weight, value_weight, q_gain, k_gain, nbr_owner, nbr_slot):
    cos, sin = rope_tables()
    hbm = pl.BlockSpec(memory_space=pl.ANY)
    smem = pl.BlockSpec(memory_space=pltpu.SMEM)
    dma = pltpu.SemaphoreType.DMA
    vmem = pltpu.VMEM
    return pl.pallas_call(
        kernel,
        out_shape=(
            jax.ShapeDtypeStruct((256, 1024), BF16),
            jax.ShapeDtypeStruct((4, NT, 256), F32),
        ),
        in_specs=[hbm] * 9 + [smem] * 2,
        out_specs=(hbm, hbm),
        scratch_shapes=[
            vmem((256, 1024), BF16),
            vmem((256, 1024), BF16),
            vmem((1, 1024), F32),
            vmem((1, 1024), F32),
            vmem((256, DH), F32),
            vmem((256, DH), F32),
            vmem((256, 1024), BF16),
            vmem((4, 4, 64, 128), F32),
            vmem((4, 4, 4, NT, 128), BF16),
            vmem((4, 4, 4, NT, 128), BF16),
            vmem((CHUNKS, 4, 4, 128, CW), BF16),
            vmem((CHUNKS, 4, 4, 128, CW), BF16),
            vmem((2, 8, 1024, 128), BF16),
            vmem((2, SPAN, 1024), BF16),
            vmem((8, 4 * SPAN, DH), F32),
            vmem((4, 4, 2 * SPAN, 256), BF16),
            vmem((4, 4, 2 * SPAN, 256), BF16),
            vmem((4 * SPAN, 1024), F32),
            vmem((SPAN, 1024), BF16),
            vmem((SPAN, 1024), BF16),
            vmem((1024, 2 * CW), BF16),
            vmem((2, 256, CW), F32),
            vmem((2, 256, CW), BF16),
            vmem((2, 2, 4, 1024, 128), F32),
            vmem((2, 4, 1024, 128), BF16),
            vmem((2, 4, 1024, 128), BF16),
            vmem((4, 2, 256, 128), BF16),
            vmem((4, 2, 256, 128), BF16),
            vmem((4, 2, 2, 256, 128), BF16),
            vmem((4, 2, 2, 256, 128), BF16),
            vmem((4, 8, 64, 128), F32),
            vmem((4, 16, 2, 64, 128), BF16),
            vmem((4, 16, 2, 64, 128), BF16),
            pltpu.SMEM((5, 16), jnp.int32),
            dma((16,)),
            dma((6,)),
            dma((2 + CHUNKS, 2, 4, 2)),
            dma((2 + CHUNKS, 2, 4, 2)),
            dma((2, 2, 2)),
            dma((2, 2, 2)),
            dma((2, 4)),
            dma((2, 4)),
            dma((3,)),
            dma((3,)),
            dma((4, 7)),
            dma((4, 7)),
            dma((4, 16)),
            dma((4, 16)),
        ],
        compiler_params=pltpu.CompilerParams(
            collective_id=0, has_side_effects=True, vmem_limit_bytes=60 * 2**20
        ),
    )(
        queries, out_grad, nbr_states, key_weight, value_weight,
        q_gain.reshape(1, -1), k_gain.reshape(1, -1), jnp.asarray(cos), jnp.asarray(sin),
        nbr_owner.T, nbr_slot.T,
    )


def solution(mesh):
    in_specs = (
        P("ctx", "enc"),
        P("ctx", "enc"),
        P("ctx", None, "enc"),
        P("ctx", "enc"),
        P("ctx", "enc"),
        P("enc"),
        P("enc"),
        P(),
        P(),
    )
    out_specs = (P("ctx", "enc"), P("ctx", None, "enc"))
    return jax.shard_map(shards, mesh=mesh, in_specs=in_specs, out_specs=out_specs, check_vma=False)
```

time: 155 us -> 131 us (0.85)
  Pallas kernels: 149 us -> 128 us
  local copies, waits for them, and re-layouts: 4.82 us -> 2.72 us
    pallas_call x1, Pallas kernels: 149 us -> 128 us  [shards(): pl.pallas_call(kernel, out_shape=(jax.ShapeDtypeStruct((256, 1024), BF16)...]
    unnamed x10 -> x4, local copies, waits for them, and re-layouts: 4.82 us -> 2.72 us
where the time goes in v2:
time: 131 us
  Pallas kernels  128 us (98%)
  local copies, waits for them, and re-layouts  2.72 us (2%)
    pallas_call x1, Pallas kernels, shards(): pl.pallas_call(kernel, out_shape=(jax.ShapeDtypeStruct((256, 1024), BF16)...  128 us
    unnamed x4, local copies, waits for them, and re-layouts  2.72 us

profile of v2, /device:TPU:1, one launch (start us, length us, event | category | flops | bytes accessed | tf_op | source)
XLA Modules:
  0.0 131.1 jit_solution(990216590323230766)
XLA Ops:
  0.6 127.7 %shard_map.122 = (bf16[256,1024]{1,0:T(8,128)(2,1)}, f32[4,128,256]{2,1,0:T(8,128)}) custom-call(bf16[256,1024]{1,0:T(8,128)(2,1)} %q_hbm.1, bf16[256,1024]{1,0:T(8,128)(2,1)} %do_hbm.1, bf16[4,128,256]{2,1,0:T(8,128)(2,1)} %pool_hbm.1, bf16[128,1024]{1,0:T(8,128)(2,1)} %kw_hbm.1, bf16[128,1024]{1,0:T(8,128)(2,1)} %vw_hbm.1, f32[1,1024]{1,0:T(1,128)} %bitcast.4, ...), custom_call_target="tpu_custom_call" | custom-call | tf_op jit(solution)/shard_map/pallas_call | solution.py:532
  128.4 0.0 copy-start
  128.4 1.9 %copy.15 = bf16[256,1024]{1,0:T(8,128)(2,1)} copy(bf16[256,1024]{1,0:T(8,128)(2,1)} %get-tuple-element.4) | data formatting | bytes 1048576
  130.3 0.0 copy-done
  130.3 0.8 copy.16
Async XLA Ops:
  128.4 1.9 %copy-start = (f32[4,128,256]{2,1,0:T(8,128)S(1)}, f32[4,128,256]{2,1,0:T(8,128)}, u32[]{:S(2)}) copy-start(f32[4,128,256]{2,1,0:T(8,128)} %get-tuple-element.5) | copy-start | bytes 1572868

commit v3 on v2

--- a/solution.py
+++ b/solution.py
@@ -57,12 +57,12 @@
 
 
 def kernel(
-    q_hbm, do_hbm, pool_hbm, kw_hbm, vw_hbm, qg_hbm, kg_hbm, cos_hbm, sin_hbm, owner_ref, slot_ref,
+    q_hbm, do_hbm, pool_hbm, kw_hbm, vw_hbm, qg_hbm, kg_hbm, cos_hbm, sin_hbm, owner_hbm, slot_hbm,
     qgrad_hbm, sgrad_hbm,
     q_ref, do_ref, qg_ref, kg_ref, cos_ref, sin_ref, qgrad_ref, sgrad_ref,
-    pool_lo, pool_hi, kw_all, vw_all, ebuf, halo, qwin, qbd, dobd, dqwin, qback_out, qback, dkv, kps, vps,
-    acc, sib_out, sib_in, t_out, t_in, m_out, m_in, refg, ret_out, ret_in, stab,
-    in_s, out_s, ag_s, ag_r, e_s, e_r, sib_s, sib_r, h_s, h_r, rs_s, rs_r, a2a_s, a2a_r,
+    line, gt_out, gt_in, gm_out, gm_in, kw_all, vw_all, ebuf, halo, qwin, qbd, dobd, dqwin, qback_out, qback, dkv, kps, vps,
+    acc, sib_out, sib_in, t_out, t_in, m_out, m_in, refg, ret_out, ret_in, stab, owner_ref, slot_ref,
+    in_s, out_s, w_s, w_r, g_s, g_r, e_s, e_r, h_s, h_r, rs_s, rs_r, ret_s, ret_r,
 ):
     c, e = lax.axis_index("ctx"), lax.axis_index("enc")
     z, x = c // 4, c % 4
@@ -70,33 +70,38 @@
     up, dn, opp = (y + 1) % 4, (y + 3) % 4, (y + 2) % 4
     enc = lambda y_, core_: y_ * 2 + core_
     other = (c, enc(y, 1 - core))
-    pool_all = (pool_lo, pool_hi)
-    pending = []
-
-    def send(src, dst, ssem, rsem, dev):
-        cp = pltpu.make_async_remote_copy(
+
+    def descriptor(src, dst, ssem, rsem, dev):
+        return pltpu.make_async_remote_copy(
             src_ref=src, dst_ref=dst, send_sem=ssem, recv_sem=rsem, device_id=dev, device_id_type=MESH
         )
+
+    def send(src, dst, ssem, rsem, dev):
+        descriptor(src, dst, ssem, rsem, dev).start()
+
+    def landed(ref, sem):
+        descriptor(ref, ref, sem, sem, other).wait_recv()
+
+    def sent(ref, sem):
+        descriptor(ref, ref, sem, sem, other).wait_send()
+
+    def load(src, dst, i):
+        cp = pltpu.make_async_copy(src, dst, in_s.at[i])
         cp.start()
-        pending.append(cp)
         return cp
 
-    loads = []
-
-    def load(src, dst):
-        cp = pltpu.make_async_copy(src, dst, in_s.at[len(loads)])
-        cp.start()
-        loads.append(cp)
-        return cp
-
-    in_pool = [load(pool_hbm.at[:, :, pl.ds(128 * f, 128)], pool_all[f].at[z, x]) for f in range(2)]
-    in_q = [load(q_hbm, q_ref), load(do_hbm, do_ref)]
+    in_pool = [
+        load(pool_hbm.at[:, :, pl.ds(128 * f, 128)], line.at[f, (x, z)[f]], f) for f in range(2)
+    ]
+    in_small = [load(owner_hbm, owner_ref, 2), load(slot_hbm, slot_ref, 3)]
     in_w = [
-        [load(src.at[:, pl.ds(j * CW, CW)], dst.at[j, z, x]) for src, dst in ((kw_hbm, kw_all), (vw_hbm, vw_all))]
+        [load(src.at[:, pl.ds(j * CW, CW)], dst.at[j, z, x], 4 + 2 * j + i) for i, (src, dst) in enumerate(((kw_hbm, kw_all), (vw_hbm, vw_all)))]
         for j in range(CHUNKS)
     ]
-    in_small = [
-        load(src, dst) for src, dst in ((qg_hbm, qg_ref), (kg_hbm, kg_ref), (cos_hbm, cos_ref), (sin_hbm, sin_ref))
+    in_q = [load(q_hbm, q_ref, 12), load(do_hbm, do_ref, 13)]
+    in_small += [
+        load(src, dst, 14 + i)
+        for i, (src, dst) in enumerate(((qg_hbm, qg_ref), (kg_hbm, kg_ref), (cos_hbm, cos_ref), (sin_hbm, sin_ref)))
     ]
 
     barrier = pltpu.get_barrier_semaphore()
@@ -106,20 +111,17 @@
         pl.semaphore_signal(barrier, inc=1, device_id=(c, there), device_id_type=MESH)
     pl.semaphore_wait(barrier, 18)
 
-    class Item:
-        def __init__(self, n, bufs, blocks=None):
-            self.n, self.bufs, self.blocks = n, bufs, blocks
-            self.cp = {}
+    class Chunk:
+        def __init__(self, j):
+            self.j = j
 
         def view(self, ab, first, second):
             zi, xi = (second, first) if ab == 0 else (first, second)
-            ref = self.bufs[ab]
-            return ref.at[zi, xi] if self.blocks is None else ref.at[zi, xi, self.blocks[ab]]
+            return (kw_all, vw_all)[ab].at[self.j, zi, xi]
 
         def half(self, ab, first, second, h):
             zi, xi = (second, first) if ab == 0 else (first, second)
-            part = pl.ds(64 * h, 64) if self.blocks is None else pl.ds(self.blocks[ab].start + h, 1)
-            return self.bufs[ab].at[zi, xi, part]
+            return (kw_all, vw_all)[ab].at[self.j, zi, xi, pl.ds(64 * h, 64)]
 
         def coords(self, ab):
             return (x, z) if ab == 0 else (z, x)
@@ -127,76 +129,119 @@
         def dev(self, ab, first, second):
             return (second * 4 + first, e) if ab == 0 else (first * 4 + second, e)
 
-        def go(self, step, ab, d, ref, to):
-            self.cp[step, ab, d] = send(
-                ref, ref, ag_s.at[self.n, ab, step, d], ag_r.at[self.n, ab, step, d], to
-            )
+        def go(self, step, ref, to):
+            send(ref, ref, w_s.at[step], w_r.at[self.j, step], to)
+
+        def got(self, step):
+            block = kw_all.at[self.j]
+            landed((block.at[0], block.at[0, pl.ds(0, 2)], block, block.at[pl.ds(0, 2)])[step], w_r.at[self.j, step])
 
         def s1(self):
             for ab in (0, 1):
                 f, s = self.coords(ab)
                 for d in (0, 1):
-                    self.go(0, ab, d, self.view(ab, f, s), self.dev(ab, (f + (1, 3)[d]) % 4, s))
+                    self.go(0, self.view(ab, f, s), self.dev(ab, (f + (1, 3)[d]) % 4, s))
 
         def s2(self):
+            self.got(0)
             for ab in (0, 1):
                 f, s = self.coords(ab)
                 for d in (0, 1):
-                    self.cp[0, ab, d].wait_recv()
                     to = self.dev(ab, (f + (1, 3)[d]) % 4, s)
-                    self.go(1, ab, d, self.half(ab, (f + (3, 1)[d]) % 4, s, d), to)
+                    self.go(1, self.half(ab, (f + (3, 1)[d]) % 4, s, d), to)
 
         def s3(self):
+            self.got(1)
             for ab in (0, 1):
                 f, s = self.coords(ab)
                 for d in (0, 1):
-                    self.cp[1, ab, d].wait_recv()
-                for d in (0, 1):
-                    to = self.dev(ab, f, (s + (1, 3)[d]) % 4)
-                    self.go(2, ab, d, self.view(ab, pl.ds(0, 4), s), to)
+                    self.go(2, self.view(ab, pl.ds(0, 4), s), self.dev(ab, f, (s + (1, 3)[d]) % 4))
 
         def s4(self):
+            self.got(2)
             for ab in (0, 1):
                 f, s = self.coords(ab)
                 for d in (0, 1):
-                    self.cp[2, ab, d].wait_recv()
                     to = self.dev(ab, f, (s + (1, 3)[d]) % 4)
-                    self.go(3, ab, d, self.view(ab, pl.ds(2 * d, 2), (s + (3, 1)[d]) % 4), to)
+                    self.go(3, self.view(ab, pl.ds(2 * d, 2), (s + (3, 1)[d]) % 4), to)
 
         def done(self):
-            for ab in (0, 1):
-                for d in (0, 1):
-                    self.cp[3, ab, d].wait_recv()
-
-    stored = (pl.ds(0, 2), pl.ds(2, 2))
-    pool = [Item(f, (pool_all[f], pool_all[f]), stored) for f in range(2)]
-    w = [Item(2 + j, (kw_all.at[j], vw_all.at[j])) for j in range(CHUNKS)]
-
-    for f in range(2):
-        in_pool[f].wait()
-        pool[f].s1()
+            self.got(3)
+
+    def ahead(f, first, second):
+        return (second * 4 + first, e) if f == 0 else (first * 4 + second, e)
+
+    def referred(f, second, r):
+        to = ahead(f, (x, z)[f], second)[0]
+        o, n = owner_ref[r % 2, to * 4 + r // 2], slot_ref[r % 2, to * 4 + r // 2]
+        first, there = (o % 4, o // 4) if f == 0 else (o // 4, o % 4)
+        block = line[f, first, n]
+        return jnp.where(there == (z, x)[f], block, jnp.zeros_like(block))
+
+    def pool1():
+        for f in range(2):
+            a, b = ((x, z), (z, x))[f]
+            for d in (0, 1):
+                ref = line.at[f, a]
+                send(ref, ref, g_s.at[0], g_r.at[0], ahead(f, (a + (1, 3)[d]) % 4, b))
+
+    def pool2():
+        landed(line.at[0], g_r.at[0])
+        for f in range(2):
+            a, b = ((x, z), (z, x))[f]
+            for d in (0, 1):
+                ref = line.at[f, (a + (3, 1)[d]) % 4, pl.ds(2 * d, 2)]
+                send(ref, ref, g_s.at[1], g_r.at[1], ahead(f, (a + (1, 3)[d]) % 4, b))
+
+    def pool3():
+        landed(line.at[0, pl.ds(0, 2)], g_r.at[1])
+        for f in range(2):
+            a, b = ((x, z), (z, x))[f]
+            for d in (0, 1):
+                for r in range(4):
+                    gt_out[f, d, r] = referred(f, (b + 2) % 4, 4 * d + r)
+                send(gt_out.at[f, d], gt_in.at[f, d], g_s.at[2], g_r.at[2], ahead(f, a, (b + (1, 3)[d]) % 4))
+        for f in range(2):
+            a, b = ((x, z), (z, x))[f]
+            for d in (0, 1):
+                to = (b + (1, 3)[d]) % 4
+                part = pl.ds(4 * (1 - d), 4)
+                for r in range(4):
+                    gm_out[f, d, 4 * (1 - d) + r] = referred(f, to, 4 * (1 - d) + r)
+                send(gm_out.at[f, d, part], gm_in.at[f, d, part], g_s.at[3], g_r.at[3], ahead(f, a, to))
+
+    def pool4():
+        landed(gt_in, g_r.at[2])
+        for f in range(2):
+            a, b = ((x, z), (z, x))[f]
+            for d in (0, 1):
+                to = (b + (1, 3)[d]) % 4
+                part = pl.ds(4 * d, 4)
+                for r in range(4):
+                    gm_out[f, d, 4 * d + r] = referred(f, to, 4 * d + r) + gt_in[f, d, r]
+                send(gm_out.at[f, d, part], gm_in.at[f, d, part], g_s.at[3], g_r.at[3], ahead(f, a, to))
+
+    w = [Chunk(j) for j in range(CHUNKS)]
+
+    for cp in in_pool:
+        cp.wait()
+    pool1()
     for cp in in_w[0]:
         cp.wait()
     w[0].s1()
     for cp in in_q:
         cp.wait()
-    halo_cps = [
-        send(src.at[pl.ds(0, SPAN)], halo.at[i], h_s.at[i], h_r.at[i], ((c + 15) % 16, e))
-        for i, src in enumerate((q_ref, do_ref))
-    ]
-    pool[0].s2()
+    for i, src in enumerate((q_ref, do_ref)):
+        send(src.at[pl.ds(0, SPAN)], halo.at[i], h_s.at[0], h_r.at[0], ((c + 15) % 16, e))
+    pool2()
     for pair in in_w[1:]:
         for cp in pair:
             cp.wait()
-    w[2].s1()
-    pool[1].s2()
-    pool[0].s3()
-    pool[1].s3()
-    w[3].s1()
+    for cp in in_small:
+        cp.wait()
     w[0].s2()
     w[1].s1()
-    for cp in in_small:
-        cp.wait()
+    pool3()
 
     def table(p, _):
         first, last, count = jnp.int32(0), jnp.int32(0), jnp.int32(0)
@@ -218,8 +263,7 @@
 
     lax.fori_loop(0, 16, table, 0)
 
-    for cp in halo_cps:
-        cp.wait_recv()
+    landed(halo, h_r.at[0])
     keep = jnp.where(c == 15, 0.0, 1.0)
     first_row = lax.broadcasted_iota(jnp.int32, (4 * SPAN, DH), 0) == 0
 
@@ -251,58 +295,58 @@
             dobd[j, s, rows, mine] = dov[r]
             dobd[j, s, rows, rest] = zero
 
-    for h in range(8):
+    for h in range(4):
         prepare(h)
-    pool[0].s4()
-
-    ring, sib = {}, {}
-
-    def to_sibling(f, i, slot):
+    pool4()
+    w[0].s3()
+    for h in range(4, 8):
+        prepare(h)
+
+
+    def to_sibling(f, slot):
         ref = ebuf.at[f, slot]
-        sib[f, i] = send(ref, ref, sib_s.at[f, i], sib_r.at[f, i], other)
+        send(ref, ref, e_s.at[2], e_r.at[f, 2], other)
 
     def y1(f):
+        b = (z, x)[f]
         for r in range(8):
-            o, n = owner_ref[r % 2, c * 4 + r // 2], slot_ref[r % 2, c * 4 + r // 2]
-            ebuf[f, e, r * NT : (r + 1) * NT, :] = pool_all[f][o // 4, o % 4, n]
-        for d, to in ((0, up), (1, dn)):
+            ebuf[f, e, r * NT : (r + 1) * NT, :] = referred(f, b, r) + gm_in[f, 0, r] + gm_in[f, 1, r]
+        for to in (up, dn):
             ref = ebuf.at[f, e]
-            ring[f, 0, d] = send(ref, ref, e_s.at[f, 0, d], e_r.at[f, 0, d], (c, enc(to, core)))
-        to_sibling(f, 0, e)
+            send(ref, ref, e_s.at[0], e_r.at[f, 0], (c, enc(to, core)))
+        to_sibling(f, e)
 
     def y2(f):
+        landed(ebuf.at[f, pl.ds(0, 2)], e_r.at[f, 0])
         for d, frm, to in ((0, dn, up), (1, up, dn)):
-            ring[f, 0, d].wait_recv()
             slot = enc(frm, core)
             part = ebuf.at[f, slot, pl.ds(512 * d, 512)]
-            ring[f, 1, d] = send(part, part, e_s.at[f, 1, d], e_r.at[f, 1, d], (c, enc(to, core)))
-            to_sibling(f, 1 + d, slot)
+            send(part, part, e_s.at[1], e_r.at[f, 1], (c, enc(to, core)))
+            to_sibling(f, slot)
 
     def y3(f):
-        for d in (0, 1):
-            ring[f, 1, d].wait_recv()
-        to_sibling(f, 3, enc(opp, core))
-
-    pool[1].s4()
-    w[0].s3()
-    pool[0].done()
+        landed(ebuf.at[f, 0], e_r.at[f, 1])
+        to_sibling(f, enc(opp, core))
+
+    landed(gm_in, g_r.at[3])
     y1(0)
+    y1(1)
     w[1].s2()
-    w[3].s2()
+    w[3].s1()
+    w[2].s1()
+    w[1].s3()
     w[2].s2()
-    pool[1].done()
-    y1(1)
+    y2(0)
     w[0].s4()
-    w[1].s3()
-    y2(0)
+    y2(1)
     w[2].s3()
-    y2(1)
     y3(0)
     y3(1)
+    w[1].s4()
+    w[3].s2()
     w[0].done()
     for f in range(2):
-        for i in range(4):
-            sib[f, i].wait_recv()
+        landed(ebuf.at[f, pl.ds(0, 4)], e_r.at[f, 2])
 
     def project(j, s):
         rows = slice(s * 256, (s + 1) * 256)
@@ -387,13 +431,12 @@
             qback_out[:, cols] = back[3 * SPAN :]
 
     compute(0, 0)
-    w[1].s4()
     compute(0, 1)
     w[2].s4()
     products(0)
-    w[3].s3()
     w[1].done()
     compute(1, 0)
+    w[3].s3()
     compute(1, 1)
     products(1)
     query_rows(0)
@@ -408,10 +451,8 @@
     compute(3, 0)
     compute(3, 1)
 
-    rs_cp = {}
-
     def rs_send(p, k, src, dst, to):
-        rs_cp[p, k] = send(src, dst, rs_s.at[p, k], rs_r.at[p, k], to)
+        send(src, dst, rs_s.at[k], rs_r.at[p, k], to)
 
     def rs_a(f):
         product(CHUNKS - 1, f, 0)
@@ -427,24 +468,22 @@
     sides = ((0, up), (1, dn))
 
     def rs_b(p):
-        rs_cp[p, 0].wait_recv()
+        landed(sib_in.at[p // 2, :, pl.ds(512 * (p % 2), 512)], rs_r.at[p, 0])
         for d, to in sides:
             t_out[p, d] = both(p, opp, 256 * d, 256).astype(BF16)
-            rs_send(p, 1 + d, t_out.at[p, d], t_in.at[p, d], (c, enc(to, core)))
+            rs_send(p, 1, t_out.at[p, d], t_in.at[p, d], (c, enc(to, core)))
         for d, to in sides:
             m_out[p, d, 1 - d] = both(p, to, 256 * (1 - d), 256).astype(BF16)
-            rs_send(p, 3 + d, m_out.at[p, d, 1 - d], m_in.at[p, d, 1 - d], (c, enc(to, core)))
+            rs_send(p, 2, m_out.at[p, d, 1 - d], m_in.at[p, d, 1 - d], (c, enc(to, core)))
 
     def rs_c(p):
+        landed(t_in.at[p], rs_r.at[p, 1])
         for d, to in sides:
-            mine = both(p, to, 256 * d, 256)
-            rs_cp[p, 1 + d].wait_recv()
-            m_out[p, d, d] = (mine + t_in[p, d].astype(F32)).astype(BF16)
-            rs_send(p, 5 + d, m_out.at[p, d, d], m_in.at[p, d, d], (c, enc(to, core)))
+            m_out[p, d, d] = (both(p, to, 256 * d, 256) + t_in[p, d].astype(F32)).astype(BF16)
+            rs_send(p, 2, m_out.at[p, d, d], m_in.at[p, d, d], (c, enc(to, core)))
 
     def rs_d(p):
-        for k in range(3, 7):
-            rs_cp[p, k].wait_recv()
+        landed(m_in.at[p], rs_r.at[p, 2])
         for h in range(2):
             total = both(p, y, 256 * h, 256) + m_in[p, 0, h].astype(F32) + m_in[p, 1, h].astype(F32)
             refg[p, 4 * h : 4 * h + 4] = total.reshape(4, 64, 128)
@@ -461,9 +500,7 @@
                 continue
             ret_out[p, d, 0] = block0
             ret_out[p, d, 1] = block1
-            rs_cp[p, 7, d] = send(
-                ret_out.at[p, d], ret_in.at[p, c], a2a_s.at[p, d], a2a_r.at[p, d], (to, e)
-            )
+            send(ret_out.at[p, d], ret_in.at[p, c], ret_s.at[0], ret_r.at[p], (to, e))
 
     outs = []
 
@@ -473,8 +510,7 @@
         outs.append(cp)
 
     def rs_e(p):
-        for d in range(1, 16):
-            rs_cp[p, 7, d].wait_recv()
+        landed(ret_in.at[p, pl.ds(0, 15)], ret_r.at[p])
 
         def add(o, sums):
             b0, b1 = ret_in[p, o, 0].astype(F32), ret_in[p, o, 1].astype(F32)
@@ -491,7 +527,7 @@
     rs_a(0)
     rs_b(0)
     query_rows(3)
-    qback_cp = send(qback_out, qback, h_s.at[2], h_r.at[2], ((c + 1) % 16, e))
+    send(qback_out, qback, h_s.at[1], h_r.at[1], ((c + 1) % 16, e))
     rs_c(0)
     rs_b(1)
     rs_d(0)
@@ -506,7 +542,7 @@
     rs_c(3)
     rs_d(3)
 
-    qback_cp.wait_recv()
+    landed(qback, h_r.at[1])
     live = jnp.where(c == 0, 0.0, 1.0)
     last_row = lax.broadcasted_iota(jnp.int32, (SPAN, DH), 0) == SPAN - 1
     for h in range(8):
@@ -519,14 +555,22 @@
         rs_e(p)
     for cp in outs:
         cp.wait()
-    for cp in pending:
-        cp.wait_send()
+    sent(halo, h_s.at[0])
+    sent(qback, h_s.at[1])
+    for step, ref in enumerate((line.at[0], line.at[0, pl.ds(0, 2)], gt_out, gm_out)):
+        sent(ref, g_s.at[step])
+    for step, ref in enumerate((kw_all.at[0], kw_all.at[0, pl.ds(0, 2)], kw_all, kw_all.at[pl.ds(0, 2)])):
+        sent(ref, w_s.at[step])
+    for step, ref in enumerate((ebuf.at[0, pl.ds(0, 4)], ebuf.at[0, pl.ds(0, 2)], ebuf.at[0])):
+        sent(ref, e_s.at[step])
+    for step, ref in enumerate((sib_out, t_out, m_out)):
+        sent(ref, rs_s.at[step])
+    sent(ret_out.at[:, pl.ds(0, 15)], ret_s.at[0])
 
 
 def shards(queries, out_grad, nbr_states, key_weight, value_weight, q_gain, k_gain, nbr_owner, nbr_slot):
     cos, sin = rope_tables()
     hbm = pl.BlockSpec(memory_space=pl.ANY)
-    smem = pl.BlockSpec(memory_space=pltpu.SMEM)
     dma = pltpu.SemaphoreType.DMA
     vmem = pltpu.VMEM
     return pl.pallas_call(
@@ -535,7 +579,7 @@
             jax.ShapeDtypeStruct((256, 1024), BF16),
             jax.ShapeDtypeStruct((4, NT, 256), F32),
         ),
-        in_specs=[hbm] * 9 + [smem] * 2,
+        in_specs=[hbm] * 11,
         out_specs=(hbm, hbm),
         scratch_shapes=[
             vmem((256, 1024), BF16),
@@ -546,8 +590,11 @@
             vmem((256, DH), F32),
             vmem((256, 1024), BF16),
             vmem((4, 4, 64, 128), F32),
-            vmem((4, 4, 4, NT, 128), BF16),
-            vmem((4, 4, 4, NT, 128), BF16),
+            vmem((2, 4, 4, NT, 128), BF16),
+            vmem((2, 2, 4, NT, 128), BF16),
+            vmem((2, 2, 4, NT, 128), BF16),
+            vmem((2, 2, 8, NT, 128), BF16),
+            vmem((2, 2, 8, NT, 128), BF16),
             vmem((CHUNKS, 4, 4, 128, CW), BF16),
             vmem((CHUNKS, 4, 4, 128, CW), BF16),
             vmem((2, 8, 1024, 128), BF16),
@@ -572,20 +619,22 @@
             vmem((4, 16, 2, 64, 128), BF16),
             vmem((4, 16, 2, 64, 128), BF16),
             pltpu.SMEM((5, 16), jnp.int32),
-            dma((16,)),
+            pltpu.SMEM((2, 64), jnp.int32),
+            pltpu.SMEM((2, 64), jnp.int32),
+            dma((18,)),
             dma((6,)),
-            dma((2 + CHUNKS, 2, 4, 2)),
-            dma((2 + CHUNKS, 2, 4, 2)),
-            dma((2, 2, 2)),
-            dma((2, 2, 2)),
-            dma((2, 4)),
-            dma((2, 4)),
+            dma((4,)),
+            dma((CHUNKS, 4)),
+            dma((4,)),
+            dma((4,)),
             dma((3,)),
+            dma((2, 3)),
+            dma((2,)),
+            dma((2,)),
             dma((3,)),
-            dma((4, 7)),
-            dma((4, 7)),
-            dma((4, 16)),
-            dma((4, 16)),
+            dma((4, 3)),
+            dma((1,)),
+            dma((4,)),
         ],
         compiler_params=pltpu.CompilerParams(
             collective_id=0, has_side_effects=True, vmem_limit_bytes=60 * 2**20

time: 131 us -> 121 us (0.924)
  Pallas kernels: 128 us -> 118 us
    pallas_call x1, Pallas kernels: 128 us -> 118 us  [shards(): pl.pallas_call(kernel, out_shape=(jax.ShapeDtypeStruct((256, 1024), BF16)...]
where the time goes in v3:
time: 121 us
  Pallas kernels  118 us (98%)
  local copies, waits for them, and re-layouts  2.72 us (2%)
    pallas_call x1, Pallas kernels, shards(): pl.pallas_call(kernel, out_shape=(jax.ShapeDtypeStruct((256, 1024), BF16)...  118 us
    unnamed x4, local copies, waits for them, and re-layouts  2.72 us

profile of v3, /device:TPU:1, one launch (start us, length us, event | category | flops | bytes accessed | tf_op | source)
XLA Modules:
  0.0 121.3 jit_solution(2592083637661589250)
XLA Ops:
  0.6 117.9 %shard_map.122 = (bf16[256,1024]{1,0:T(8,128)(2,1)}, f32[4,128,256]{2,1,0:T(8,128)}) custom-call(bf16[256,1024]{1,0:T(8,128)(2,1)} %q_hbm.1, bf16[256,1024]{1,0:T(8,128)(2,1)} %do_hbm.1, bf16[4,128,256]{2,1,0:T(8,128)(2,1)} %pool_hbm.1, bf16[128,1024]{1,0:T(8,128)(2,1)} %kw_hbm.1, bf16[128,1024]{1,0:T(8,128)(2,1)} %vw_hbm.1, f32[1,1024]{1,0:T(1,128)} %bitcast.4, ...), custom_call_target="tpu_custom_call" | custom-call | tf_op jit(solution)/shard_map/pallas_call | solution.py:576
  118.6 0.0 copy-start
  118.6 1.9 %copy.15 = bf16[256,1024]{1,0:T(8,128)(2,1)} copy(bf16[256,1024]{1,0:T(8,128)(2,1)} %get-tuple-element.4) | data formatting | bytes 1048576
  120.5 0.0 copy-done
  120.5 0.8 copy.16
Async XLA Ops:
  118.6 1.9 %copy-start = (f32[4,128,256]{2,1,0:T(8,128)S(1)}, f32[4,128,256]{2,1,0:T(8,128)}, u32[]{:S(2)}) copy-start(f32[4,128,256]{2,1,0:T(8,128)} %get-tuple-element.5) | copy-start | bytes 1572868

commit v4 on v3

--- a/solution.py
+++ b/solution.py
@@ -336,6 +336,7 @@
     w[2].s1()
     w[1].s3()
     w[2].s2()
+    w[3].s2()
     y2(0)
     w[0].s4()
     y2(1)
@@ -343,7 +344,6 @@
     y3(0)
     y3(1)
     w[1].s4()
-    w[3].s2()
     w[0].done()
     for f in range(2):
         landed(ebuf.at[f, pl.ds(0, 4)], e_r.at[f, 2])
@@ -434,9 +434,9 @@
     compute(0, 1)
     w[2].s4()
     products(0)
+    w[3].s3()
     w[1].done()
     compute(1, 0)
-    w[3].s3()
     compute(1, 1)
     products(1)
     query_rows(0)
@@ -486,14 +486,13 @@
         landed(m_in.at[p], rs_r.at[p, 2])
         for h in range(2):
             total = both(p, y, 256 * h, 256) + m_in[p, 0, h].astype(F32) + m_in[p, 1, h].astype(F32)
-            refg[p, 4 * h : 4 * h + 4] = total.reshape(4, 64, 128)
+            refg[p, 4 * h : 4 * h + 4] = total.astype(BF16).reshape(4, 64, 128)
         for d in range(16):
             to = (c + d) % 16
             count = stab[2, to]
-            one = jnp.where(count > 0, 1.0, 0.0)
-            two = jnp.where(count > 1, 1.0, 0.0)
-            block0 = (refg[p, stab[0, to]] * one).astype(BF16)
-            block1 = (refg[p, stab[1, to]] * two).astype(BF16)
+            none = jnp.zeros((64, 128), BF16)
+            block0 = jnp.where(count > 0, refg[p, stab[0, to]], none)
+            block1 = jnp.where(count > 1, refg[p, stab[1, to]], none)
             if d == 0:
                 ret_in[p, c, 0] = block0
                 ret_in[p, c, 1] = block1
@@ -528,18 +527,18 @@
     rs_b(0)
     query_rows(3)
     send(qback_out, qback, h_s.at[1], h_r.at[1], ((c + 1) % 16, e))
+    rs_a(1)
     rs_c(0)
     rs_b(1)
     rs_d(0)
     rs_c(1)
-    rs_a(1)
+    rs_b(2)
     rs_d(1)
-    rs_b(2)
     rs_c(2)
     rs_b(3)
-    store(qgrad_ref.at[pl.ds(SPAN, 3 * SPAN)], qgrad_hbm.at[pl.ds(SPAN, 3 * SPAN)])
     rs_d(2)
     rs_c(3)
+    store(qgrad_ref.at[pl.ds(SPAN, 3 * SPAN)], qgrad_hbm.at[pl.ds(SPAN, 3 * SPAN)])
     rs_d(3)
 
     landed(qback, h_r.at[1])
@@ -615,7 +614,7 @@
             vmem((4, 2, 256, 128), BF16),
             vmem((4, 2, 2, 256, 128), BF16),
             vmem((4, 2, 2, 256, 128), BF16),
-            vmem((4, 8, 64, 128), F32),
+            vmem((4, 8, 64, 128), BF16),
             vmem((4, 16, 2, 64, 128), BF16),
             vmem((4, 16, 2, 64, 128), BF16),
             pltpu.SMEM((5, 16), jnp.int32),

time: 121 us -> 119 us (0.983)
  Pallas kernels: 118 us -> 116 us
    pallas_call x1, Pallas kernels: 118 us -> 116 us  [shards(): pl.pallas_call(kernel, out_shape=(jax.ShapeDtypeStruct((256, 1024), BF16)...]
where the time goes in v4:
time: 119 us
  Pallas kernels  116 us (97%)
  local copies, waits for them, and re-layouts  2.72 us (2%)
    pallas_call x1, Pallas kernels, shards(): pl.pallas_call(kernel, out_shape=(jax.ShapeDtypeStruct((256, 1024), BF16)...  116 us
    unnamed x4, local copies, waits for them, and re-layouts  2.72 us

profile of v4, /device:TPU:1, one launch (start us, length us, event | category | flops | bytes accessed | tf_op | source)
XLA Modules:
  0.0 119.0 jit_solution(11600316262753369337)
XLA Ops:
  0.6 115.6 %shard_map.122 = (bf16[256,1024]{1,0:T(8,128)(2,1)}, f32[4,128,256]{2,1,0:T(8,128)}) custom-call(bf16[256,1024]{1,0:T(8,128)(2,1)} %q_hbm.1, bf16[256,1024]{1,0:T(8,128)(2,1)} %do_hbm.1, bf16[4,128,256]{2,1,0:T(8,128)(2,1)} %pool_hbm.1, bf16[128,1024]{1,0:T(8,128)(2,1)} %kw_hbm.1, bf16[128,1024]{1,0:T(8,128)(2,1)} %vw_hbm.1, f32[1,1024]{1,0:T(1,128)} %bitcast.4, ...), custom_call_target="tpu_custom_call" | custom-call | tf_op jit(solution)/shard_map/pallas_call | solution.py:575
  116.3 0.0 copy-start
  116.3 1.9 %copy.15 = bf16[256,1024]{1,0:T(8,128)(2,1)} copy(bf16[256,1024]{1,0:T(8,128)(2,1)} %get-tuple-element.4) | data formatting | bytes 1048576
  118.2 0.0 copy-done
  118.2 0.8 copy.16
Async XLA Ops:
  116.3 1.9 %copy-start = (f32[4,128,256]{2,1,0:T(8,128)S(1)}, f32[4,128,256]{2,1,0:T(8,128)}, u32[]{:S(2)}) copy-start(f32[4,128,256]{2,1,0:T(8,128)} %get-tuple-element.5) | copy-start | bytes 1572868

commit v5 on v4

--- a/solution.py
+++ b/solution.py
@@ -58,11 +58,11 @@
 
 def kernel(
     q_hbm, do_hbm, pool_hbm, kw_hbm, vw_hbm, qg_hbm, kg_hbm, cos_hbm, sin_hbm, owner_hbm, slot_hbm,
-    qgrad_hbm, sgrad_hbm,
-    q_ref, do_ref, qg_ref, kg_ref, cos_ref, sin_ref, qgrad_ref, sgrad_ref,
-    line, gt_out, gt_in, gm_out, gm_in, kw_all, vw_all, ebuf, halo, qwin, qbd, dobd, dqwin, qback_out, qback, dkv, kps, vps,
+    qgrad_ref, sgrad_ref,
+    q_ref, do_ref, qg_ref, kg_ref, cos_ref, sin_ref,
+    line, gt_out, gt_in, gm_out, gm_in, kw_all, vw_all, ebuf, halo, qwin, qbd, dobd, dqwin, qback_out, qback, dkv, kps, vps, early,
     acc, sib_out, sib_in, t_out, t_in, m_out, m_in, refg, ret_out, ret_in, stab, owner_ref, slot_ref,
-    in_s, out_s, w_s, w_r, g_s, g_r, e_s, e_r, h_s, h_r, rs_s, rs_r, ret_s, ret_r,
+    in_s, w_s, w_r, g_s, g_r, e_s, e_r, h_s, h_r, rs_s, rs_r, ret_s, ret_r,
 ):
     c, e = lax.axis_index("ctx"), lax.axis_index("enc")
     z, x = c // 4, c % 4
@@ -348,7 +348,28 @@
     for f in range(2):
         landed(ebuf.at[f, pl.ds(0, 4)], e_r.at[f, 2])
 
+    def line_part(s, zi, xi):
+        rows = slice(s * 256, (s + 1) * 256)
+        j = CHUNKS - 1
+        e_key = jnp.concatenate([ebuf[i % 2, 2 * zi + i // 2, rows, :] for i in range(4)], axis=1)
+        e_value = jnp.concatenate([ebuf[xi % 2, 2 * i + xi // 2, rows, :] for i in range(4)], axis=1)
+        return (
+            jnp.dot(e_key, kw_all[j, zi].reshape(512, CW), preferred_element_type=F32),
+            jnp.dot(e_value, vw_all[j, :, xi].reshape(512, CW), preferred_element_type=F32),
+        )
+
+    def project_early():
+        for s in range(4):
+            parts = [line_part(s, (z + d) % 4, (x + d) % 4) for d in (0, 1, 3)]
+            early[0, s] = parts[0][0] + parts[1][0] + parts[2][0]
+            early[1, s] = parts[0][1] + parts[1][1] + parts[2][1]
+
     def project(j, s):
+        if j == CHUNKS - 1:
+            key, value = line_part(s, (z + 2) % 4, (x + 2) % 4)
+            kps[s % 2] = (early[0, s] + key).astype(BF16).astype(F32)
+            vps[s % 2] = (early[1, s] + value).astype(BF16)
+            return
         rows = slice(s * 256, (s + 1) * 256)
         ecat = jnp.concatenate([ebuf[f, i, rows, :] for i in range(8) for f in range(2)], axis=1)
         kw, vw = kw_all[j].reshape(2048, CW), vw_all[j].reshape(2048, CW)
@@ -404,19 +425,20 @@
                 project(j, s + 1)
             attend(j, s)
 
-    def product(j, f, which):
+    def product(j, f, which, start=0, size=1024):
         xi = 2 * (core if which else 1 - core) + f
         for i in range(2):
             wcat = jnp.concatenate([b[j, 2 * i : 2 * i + 2, xi].reshape(256, CW) for b in (kw_all, vw_all)], axis=1)
-            part = lax.dot_general(dkv[...], wcat, NT_DIMS, preferred_element_type=F32)
+            rows = slice(start, start + size)
+            part = lax.dot_general(dkv[rows, :], wcat, NT_DIMS, preferred_element_type=F32)
             for k in range(2):
                 new = part[:, k * 128 : (k + 1) * 128]
                 if j > 0:
-                    new = new + acc[f, which, 2 * i + k]
+                    new = new + acc[f, which, 2 * i + k, rows, :]
                 if j == CHUNKS - 1 and which == 0:
-                    sib_out[f, 2 * i + k] = new.astype(BF16)
+                    sib_out[f, 2 * i + k, rows, :] = new.astype(BF16)
                 else:
-                    acc[f, which, 2 * i + k] = new
+                    acc[f, which, 2 * i + k, rows, :] = new
 
     def products(j):
         for f in range(2):
@@ -447,6 +469,7 @@
     compute(2, 1)
     products(2)
     query_rows(2)
+    project_early()
     w[3].done()
     compute(3, 0)
     compute(3, 1)
@@ -454,12 +477,12 @@
     def rs_send(p, k, src, dst, to):
         send(src, dst, rs_s.at[k], rs_r.at[p, k], to)
 
-    def rs_a(f):
-        product(CHUNKS - 1, f, 0)
-        for h in range(2):
-            rows = pl.ds(512 * h, 512)
-            rs_send(2 * f + h, 0, sib_out.at[f, :, rows], sib_in.at[f, :, rows], other)
-        product(CHUNKS - 1, f, 1)
+    def rs_a(p):
+        f, h = p // 2, p % 2
+        product(CHUNKS - 1, f, 0, 512 * h, 512)
+        rows = pl.ds(512 * h, 512)
+        rs_send(p, 0, sib_out.at[f, :, rows], sib_in.at[f, :, rows], other)
+        product(CHUNKS - 1, f, 1, 512 * h, 512)
 
     def both(p, i, start, size):
         rows = pl.ds(512 * (p % 2) + start, size)
@@ -501,13 +524,6 @@
             ret_out[p, d, 1] = block1
             send(ret_out.at[p, d], ret_in.at[p, c], ret_s.at[0], ret_r.at[p], (to, e))
 
-    outs = []
-
-    def store(src, dst):
-        cp = pltpu.make_async_copy(src, dst, out_s.at[len(outs)])
-        cp.start()
-        outs.append(cp)
-
     def rs_e(p):
         landed(ret_in.at[p, pl.ds(0, 15)], ret_r.at[p])
 
@@ -520,8 +536,7 @@
             )
 
         for n, a in enumerate(lax.fori_loop(0, 16, add, tuple(jnp.zeros((64, 128), F32) for _ in range(4)))):
-            sgrad_ref[p, n] = a
-        store(sgrad_ref.at[p], sgrad_hbm.at[:, pl.ds(64 * (p % 2), 64), pl.ds(128 * (p // 2), 128)])
+            sgrad_ref[n, 64 * (p % 2) : 64 * (p % 2) + 64, 128 * (p // 2) : 128 * (p // 2) + 128] = a
 
     rs_a(0)
     rs_b(0)
@@ -530,15 +545,16 @@
     rs_a(1)
     rs_c(0)
     rs_b(1)
+    rs_a(2)
     rs_d(0)
     rs_c(1)
     rs_b(2)
+    rs_a(3)
     rs_d(1)
     rs_c(2)
     rs_b(3)
     rs_d(2)
     rs_c(3)
-    store(qgrad_ref.at[pl.ds(SPAN, 3 * SPAN)], qgrad_hbm.at[pl.ds(SPAN, 3 * SPAN)])
     rs_d(3)
 
     landed(qback, h_r.at[1])
@@ -548,12 +564,9 @@
         cols = slice(h * DH, (h + 1) * DH)
         head = qback[:, cols].astype(F32) * live
         qgrad_ref[0:SPAN, cols] = jnp.where(last_row, dqwin[0:1, cols], head).astype(BF16)
-    store(qgrad_ref.at[pl.ds(0, SPAN)], qgrad_hbm.at[pl.ds(0, SPAN)])
 
     for p in range(4):
         rs_e(p)
-    for cp in outs:
-        cp.wait()
     sent(halo, h_s.at[0])
     sent(qback, h_s.at[1])
     for step, ref in enumerate((line.at[0], line.at[0, pl.ds(0, 2)], gt_out, gm_out)):
@@ -572,14 +585,15 @@
     hbm = pl.BlockSpec(memory_space=pl.ANY)
     dma = pltpu.SemaphoreType.DMA
     vmem = pltpu.VMEM
+    whole = pl.BlockSpec(memory_space=pltpu.VMEM)
     return pl.pallas_call(
         kernel,
         out_shape=(
-            jax.ShapeDtypeStruct((256, 1024), BF16),
-            jax.ShapeDtypeStruct((4, NT, 256), F32),
+            vmem((256, 1024), BF16),
+            vmem((4, NT, 256), F32),
         ),
         in_specs=[hbm] * 11,
-        out_specs=(hbm, hbm),
+        out_specs=(whole, whole),
         scratch_shapes=[
             vmem((256, 1024), BF16),
             vmem((256, 1024), BF16),
@@ -587,8 +601,6 @@
             vmem((1, 1024), F32),
             vmem((256, DH), F32),
             vmem((256, DH), F32),
-            vmem((256, 1024), BF16),
-            vmem((4, 4, 64, 128), F32),
             vmem((2, 4, 4, NT, 128), BF16),
             vmem((2, 2, 4, NT, 128), BF16),
             vmem((2, 2, 4, NT, 128), BF16),
@@ -607,6 +619,7 @@
             vmem((1024, 2 * CW), BF16),
             vmem((2, 256, CW), F32),
             vmem((2, 256, CW), BF16),
+            vmem((2, 4, 256, CW), F32),
             vmem((2, 2, 4, 1024, 128), F32),
             vmem((2, 4, 1024, 128), BF16),
             vmem((2, 4, 1024, 128), BF16),
@@ -621,7 +634,6 @@
             pltpu.SMEM((2, 64), jnp.int32),
             pltpu.SMEM((2, 64), jnp.int32),
             dma((18,)),
-            dma((6,)),
             dma((4,)),
             dma((CHUNKS, 4)),
             dma((4,)),
@@ -636,7 +648,7 @@
             dma((4,)),
         ],
         compiler_params=pltpu.CompilerParams(
-            collective_id=0, has_side_effects=True, vmem_limit_bytes=60 * 2**20
+            collective_id=0, has_side_effects=True, vmem_limit_bytes=56 * 2**20
         ),
     )(
         queries, out_grad, nbr_states, key_weight, value_weight,

time: 119 us -> 116 us (0.975)
  Pallas kernels: 116 us -> 114 us
    pallas_call x1, Pallas kernels: 116 us -> 114 us  [shards(): pl.pallas_call(kernel, out_shape=(vmem((256, 1024), BF16), vmem((4, NT, 2...]
    unnamed x4 -> x2, local copies, waits for them, and re-layouts: 2.72 us -> 1.59 us
where the time goes in v5:
time: 116 us
  Pallas kernels  114 us (98%)
  local copies, waits for them, and re-layouts  1.59 us (1%)
    pallas_call x1, Pallas kernels, shards(): pl.pallas_call(kernel, out_shape=(vmem((256, 1024), BF16), vmem((4, NT, 2...  114 us

profile of v5, /device:TPU:1, one launch (start us, length us, event | category | flops | bytes accessed | tf_op | source)
XLA Modules:
  0.0 116.2 jit_solution(9613883798890560470)
XLA Ops:
  0.6 114.0 %shard_map.122 = (bf16[256,1024]{1,0:T(8,128)(2,1)S(1)}, f32[4,128,256]{2,1,0:T(8,128)S(1)}) custom-call(bf16[256,1024]{1,0:T(8,128)(2,1)} %q_hbm.1, bf16[256,1024]{1,0:T(8,128)(2,1)} %do_hbm.1, bf16[4,128,256]{2,1,0:T(8,128)(2,1)} %pool_hbm.1, bf16[128,1024]{1,0:T(8,128)(2,1)} %kw_hbm.1, bf16[128,1024]{1,0:T(8,128)(2,1)} %vw_hbm.1, f32[1,1024]{1,0:T(1,128)} %bitcast.4, ...), custom_call_target="tpu_custom_call" | custom-call | tf_op jit(solution)/shard_map/pallas_call | solution.py:589
  114.6 0.8 copy.15
  115.4 0.8 copy.16

commit v6 on v5

--- a/solution.py
+++ b/solution.py
@@ -461,14 +461,11 @@
     compute(1, 0)
     compute(1, 1)
     products(1)
-    query_rows(0)
-    query_rows(1)
     w[2].done()
     compute(2, 0)
     w[3].s4()
     compute(2, 1)
     products(2)
-    query_rows(2)
     project_early()
     w[3].done()
     compute(3, 0)
@@ -510,8 +507,8 @@
         for h in range(2):
             total = both(p, y, 256 * h, 256) + m_in[p, 0, h].astype(F32) + m_in[p, 1, h].astype(F32)
             refg[p, 4 * h : 4 * h + 4] = total.astype(BF16).reshape(4, 64, 128)
-        for d in range(16):
-            to = (c + d) % 16
+        for d in (0, 10, 9, 11, 6, 14, 5, 7, 13, 15, 8, 2, 1, 3, 4, 12):
+            to = (z + d // 4) % 4 * 4 + (x + d % 4) % 4
             count = stab[2, to]
             none = jnp.zeros((64, 128), BF16)
             block0 = jnp.where(count > 0, refg[p, stab[0, to]], none)
@@ -540,7 +537,8 @@
 
     rs_a(0)
     rs_b(0)
-    query_rows(3)
+    for j in range(CHUNKS):
+        query_rows(j)
     send(qback_out, qback, h_s.at[1], h_r.at[1], ((c + 1) % 16, e))
     rs_a(1)
     rs_c(0)

time: 116 us -> 116 us (level)
  no operation moved by 1% of the time
where the time goes in v6:
time: 116 us
  Pallas kernels  114 us (98%)
  local copies, waits for them, and re-layouts  1.59 us (1%)
    pallas_call x1, Pallas kernels, shards(): pl.pallas_call(kernel, out_shape=(vmem((256, 1024), BF16), vmem((4, NT, 2...  114 us

profile of v6, /device:TPU:1, one launch (start us, length us, event | category | flops | bytes accessed | tf_op | source)
XLA Modules:
  0.0 115.9 jit_solution(8322389928658480278)
XLA Ops:
  0.6 113.7 %shard_map.122 = (bf16[256,1024]{1,0:T(8,128)(2,1)S(1)}, f32[4,128,256]{2,1,0:T(8,128)S(1)}) custom-call(bf16[256,1024]{1,0:T(8,128)(2,1)} %q_hbm.1, bf16[256,1024]{1,0:T(8,128)(2,1)} %do_hbm.1, bf16[4,128,256]{2,1,0:T(8,128)(2,1)} %pool_hbm.1, bf16[128,1024]{1,0:T(8,128)(2,1)} %kw_hbm.1, bf16[128,1024]{1,0:T(8,128)(2,1)} %vw_hbm.1, f32[1,1024]{1,0:T(1,128)} %bitcast.4, ...), custom_call_target="tpu_custom_call" | custom-call | tf_op jit(solution)/shard_map/pallas_call | solution.py:587
  114.3 0.8 copy.15
  115.1 0.8 copy.16
